TPU v7x, 32 devices: a whole 2x2x4 slice. The times are simulated.
32 devices in a mesh: dp: 4 (over y, x), seq: 8 (over z, core).
Axes of the slice: x: 2, y: 2, z: 4, core: 2. Of those that a mesh axis runs over, the one named last changes fastest.
Arguments:
- states: bfloat16 [4, 1024, 512], P('dp', 'seq'), may hold values from -6 to 6
- w_qkv: bfloat16 [512, 1536], replicated, may hold values from -0.25 to 0.25
- qv_bias: float32 [2, 512], replicated, may hold values from -2 to 2
- output_weight: bfloat16 [512, 512], replicated, may hold values from -1 to 1
- out_bias: float32 [512], replicated, may hold values from -2 to 2
- w_up: bfloat16 [512, 2048], replicated, may hold values from -0.25 to 0.25
- up_bias: float32 [2048], replicated, may hold values from -2 to 2
- w_down: bfloat16 [2048, 512], replicated, may hold values from -0.125 to 0.125
- down_bias: float32 [512], replicated, may hold values from -2 to 2
- norm_gain: float32 [2, 512], replicated, may hold values from 0.5 to 1.5
- norm_shift: float32 [2, 512], replicated, may hold values from -2 to 2
- halt_weight: float32 [512], replicated, may hold values from -0.25 to 0.25
- halt_bias: float32 [1], replicated, may hold values from -3 to 3
- cotangent: bfloat16 [4, 1024, 512], P('dp', 'seq'), may hold values from -6 to 6
- lengths: int32 [4], P('dp'), may hold values from 1 to 1024, as said below
- caps: int32 [4, 1024], P('dp', 'seq'), may hold values from 1 to 2
Outputs:
- final_state: float32 [4, 1024, 512], P('dp', 'seq')
- input_grad: float32 [4, 1024, 512], P('dp', 'seq')
- grad_w_qkv: float32 [512, 1536], replicated
- grad_qv_bias: float32 [2, 512], replicated
- grad_w_out: float32 [512, 512], replicated
- grad_out_bias: float32 [512], replicated
- grad_w_up: float32 [512, 2048], replicated
- grad_up_bias: float32 [2048], replicated
- grad_w_down: float32 [2048, 512], replicated
- grad_down_bias: float32 [512], replicated
- grad_norm_gain: float32 [2, 512], replicated
- grad_norm_shift: float32 [2, 512], replicated
- grad_halt_weight: float32 [512], replicated
- grad_halt_bias: float32 [1], replicated
Inputs may be any that keep to these rules, and one draw needn't show every extreme that they name: `lengths`: of the 1 sequence of each index of dp, one has all 1024 positions valid.
All inputs are finite; a program needn't handle non-finite values.
Results may differ from a plain program's by a relative error of at most 0.033.
Values may be sent and summed in bfloat16 or wider, within the bound.
A program may use at most 192 MiB of HBM per device.

v0:
```python
import math

import jax
import jax.numpy as jnp
from jax import lax
from jax.sharding import PartitionSpec as P

HEADS = 8
PONDER = 2


PONDER_COST = 0.01
NORM_EPSILON = 1e-05
MASK_FILL = -1e30


def normalize(resid, gain, shift):
    centered = resid - jnp.mean(resid, axis=-1, keepdims=True)
    spread = jnp.mean(centered * centered, axis=-1, keepdims=True)
    return centered * lax.rsqrt(spread + NORM_EPSILON) * gain + shift


def halt_mix(halt_probs, caps):
    step_count = halt_probs.shape[-1] + 1
    remain = jnp.ones(caps.shape, halt_probs.dtype)
    leftover = jnp.zeros(caps.shape, halt_probs.dtype)
    columns = []
    for number in range(step_count):
        if number < step_count - 1:
            partial_weight = halt_probs[..., number] * remain
        else:
            partial_weight = jnp.zeros(caps.shape, halt_probs.dtype)
        column = jnp.where(
            caps > number + 1, partial_weight, jnp.where(caps == number + 1, remain, 0.0)
        )
        columns.append(column)
        leftover = jnp.where(caps == number + 1, remain, leftover)
        if number < step_count - 1:
            remain = remain * (1.0 - halt_probs[..., number])
    return (jnp.stack(columns, -1), leftover)


def block_of_heads(piece_rows, offset_rows, block_len, head_count):
    sliced = lax.dynamic_slice_in_dim(piece_rows, offset_rows, block_len, 1)
    return sliced.reshape(sliced.shape[0], block_len, head_count, sliced.shape[2] // head_count)


def key_mask(lengths, offset_rows, block_len):
    positions = offset_rows + jnp.arange(block_len, dtype=jnp.int32)
    return (positions[None, :] < lengths[:, None])[:, None, None, :]


def attend(queries, key_rows, value_rows, lengths, head_count):
    seq_count, shard_len, model_width = queries.shape
    head_size = model_width // head_count
    score_scale = head_size ** (-0.5)
    query_heads = queries.reshape(seq_count, shard_len, head_count, head_size)
    start_state = (
        jnp.full((seq_count, head_count, shard_len), MASK_FILL, jnp.float32),
        jnp.zeros((seq_count, head_count, shard_len), jnp.float32),
        jnp.zeros((seq_count, shard_len, head_count, head_size), jnp.float32),
    )
    key_piece = lax.all_gather(key_rows, "seq", axis=1, tiled=True)
    value_piece = lax.all_gather(value_rows, "seq", axis=1, tiled=True)
    row_count = key_piece.shape[1]
    block_len = math.gcd(row_count, 512)

    def one_block(block_index, inner):
        running_max, running_sum, weighted = inner
        offset_rows = block_index * block_len
        key_block = block_of_heads(key_piece, offset_rows, block_len, head_count)
        value_block = block_of_heads(value_piece, offset_rows, block_len, head_count)
        key_valid = key_mask(lengths, offset_rows, block_len)
        scores = (
            jnp.einsum(
                "sqhe,skhe->shqk", query_heads, key_block, preferred_element_type=jnp.float32
            )
            * score_scale
        )
        scores = jnp.where(key_valid, scores, MASK_FILL)
        new_max = jnp.maximum(running_max, jnp.max(scores, axis=-1))
        unnormed = jnp.where(key_valid, jnp.exp(scores - new_max[..., None]), 0.0)
        factor = jnp.exp(running_max - new_max)
        running_sum = running_sum * factor + jnp.sum(unnormed, axis=-1)
        update = jnp.einsum(
            "shqk,skhe->sqhe",
            unnormed.astype(jnp.bfloat16),
            value_block,
            preferred_element_type=jnp.float32,
        )
        weighted = weighted * jnp.transpose(factor, (0, 2, 1))[..., None] + update
        return (new_max, running_sum, weighted)

    running_max, running_sum, weighted = lax.fori_loop(
        0, row_count // block_len, one_block, start_state
    )
    context = (weighted / jnp.transpose(running_sum, (0, 2, 1))[..., None]).reshape(queries.shape)
    log_total = jnp.transpose(running_max + jnp.log(running_sum), (0, 2, 1))
    return (context, log_total)


def attend_back(
    queries, key_rows, value_rows, lengths, head_count, grad_context, context, log_total
):
    seq_count, shard_len, model_width = queries.shape
    head_size = model_width // head_count
    score_scale = head_size ** (-0.5)
    query_heads = queries.reshape(seq_count, shard_len, head_count, head_size)
    grad_heads = grad_context.reshape(seq_count, shard_len, head_count, head_size)
    row_dots = jnp.sum(
        grad_context.astype(jnp.float32).reshape(grad_heads.shape)
        * context.reshape(grad_heads.shape),
        axis=-1,
    )
    dots_heads = jnp.transpose(row_dots, (0, 2, 1))
    log_heads = jnp.transpose(log_total, (0, 2, 1))
    total_len = shard_len * lax.axis_size("seq")
    start_state = (
        jnp.zeros(query_heads.shape, jnp.float32),
        jnp.zeros((seq_count, total_len, model_width), jnp.float32),
        jnp.zeros((seq_count, total_len, model_width), jnp.float32),
    )
    key_piece = lax.all_gather(key_rows, "seq", axis=1, tiled=True)
    value_piece = lax.all_gather(value_rows, "seq", axis=1, tiled=True)
    row_count = key_piece.shape[1]
    block_len = math.gcd(row_count, 512)

    def one_block(block_index, inner):
        grad_query, grad_key_all, grad_value_all = inner
        offset_rows = block_index * block_len
        key_block = block_of_heads(key_piece, offset_rows, block_len, head_count)
        value_block = block_of_heads(value_piece, offset_rows, block_len, head_count)
        key_valid = key_mask(lengths, offset_rows, block_len)
        scores = (
            jnp.einsum(
                "sqhe,skhe->shqk", query_heads, key_block, preferred_element_type=jnp.float32
            )
            * score_scale
        )
        probs = jnp.where(key_valid, jnp.exp(scores - log_heads[..., None]), 0.0)
        grad_probs = jnp.einsum(
            "sqhe,skhe->shqk", grad_heads, value_block, preferred_element_type=jnp.float32
        )
        grad_scores = (probs * (grad_probs - dots_heads[..., None])).astype(jnp.bfloat16)
        grad_query = grad_query + score_scale * jnp.einsum(
            "shqk,skhe->sqhe", grad_scores, key_block, preferred_element_type=jnp.float32
        )
        key_part = score_scale * jnp.einsum(
            "shqk,sqhe->skhe", grad_scores, query_heads, preferred_element_type=jnp.float32
        )
        value_part = jnp.einsum(
            "shqk,sqhe->skhe",
            probs.astype(jnp.bfloat16),
            grad_heads,
            preferred_element_type=jnp.float32,
        )
        grad_key_all = lax.dynamic_update_slice_in_dim(
            grad_key_all, key_part.reshape(seq_count, block_len, model_width), offset_rows, 1
        )
        grad_value_all = lax.dynamic_update_slice_in_dim(
            grad_value_all, value_part.reshape(seq_count, block_len, model_width), offset_rows, 1
        )
        return (grad_query, grad_key_all, grad_value_all)

    grad_query, grad_key_all, grad_value_all = lax.fori_loop(
        0, row_count // block_len, one_block, start_state
    )
    grad_key, grad_value = (
        lax.psum_scatter(grad_key_all, "seq", scatter_dimension=1, tiled=True),
        lax.psum_scatter(grad_value_all, "seq", scatter_dimension=1, tiled=True),
    )
    return (grad_query.reshape(queries.shape), grad_key, grad_value)


def forward_block(current, weights_tuple, lengths, head_count):
    (
        w_qkv,
        qv_bias,
        output_weight,
        out_bias,
        w_up,
        up_bias,
        w_down,
        down_bias,
        norm_gain,
        norm_shift,
    ) = weights_tuple
    model_width = current.shape[-1]
    rounded = current.astype(jnp.bfloat16)
    projected = jnp.einsum("snd,df->snf", rounded, w_qkv, preferred_element_type=jnp.float32)
    queries = (projected[..., :model_width] + qv_bias[0]).astype(jnp.bfloat16)
    key_rows = projected[..., model_width : 2 * model_width].astype(jnp.bfloat16)
    value_rows = (projected[..., 2 * model_width :] + qv_bias[1]).astype(jnp.bfloat16)
    context, log_total = attend(queries, key_rows, value_rows, lengths, head_count)
    context_reduced = context.astype(jnp.bfloat16)
    resid_one = (
        current
        + jnp.einsum(
            "jry,ym->jrm", context_reduced, output_weight, preferred_element_type=jnp.float32
        )
        + out_bias
    )
    normed_one = normalize(resid_one, norm_gain[0], norm_shift[0])
    normed_low = normed_one.astype(jnp.bfloat16)
    pre_hidden = (
        jnp.einsum("snd,df->snf", normed_low, w_up, preferred_element_type=jnp.float32) + up_bias
    )
    hidden_low = jax.nn.gelu(pre_hidden).astype(jnp.bfloat16)
    resid_two = (
        normed_one
        + jnp.einsum("snf,fd->snd", hidden_low, w_down, preferred_element_type=jnp.float32)
        + down_bias
    )
    updated = normalize(resid_two, norm_gain[1], norm_shift[1])
    return {
        "rounded": rounded,
        "queries": queries,
        "key_rows": key_rows,
        "value_rows": value_rows,
        "context": context,
        "log_total": log_total,
        "context_low": context_reduced,
        "resid_one": resid_one,
        "normed_low": normed_low,
        "pre_hidden": pre_hidden,
        "hidden_low": hidden_low,
        "resid_two": resid_two,
        "updated": updated,
    }


def backward_block(grad_updated, saved_entry, weights_tuple, lengths, head_count):
    (
        w_qkv,
        qv_bias,
        output_weight,
        out_bias,
        w_up,
        up_bias,
        w_down,
        down_bias,
        norm_gain,
        norm_shift,
    ) = weights_tuple
    model_width = output_weight.shape[0]
    _, pull_two = jax.vjp(normalize, saved_entry["resid_two"], norm_gain[1], norm_shift[1])
    grad_resid_two, gain_two, shift_two = pull_two(grad_updated)
    grad_mlp = grad_resid_two.astype(jnp.bfloat16)
    grad_down_bias = jnp.sum(grad_mlp.astype(jnp.float32), axis=(0, 1))
    grad_w_down = jnp.einsum(
        "snf,snd->fd", saved_entry["hidden_low"], grad_mlp, preferred_element_type=jnp.float32
    )
    grad_hidden = jnp.einsum("snd,fd->snf", grad_mlp, w_down, preferred_element_type=jnp.float32)
    _, pull_gelu = jax.vjp(jax.nn.gelu, saved_entry["pre_hidden"])
    grad_pre = pull_gelu(grad_hidden)[0].astype(jnp.bfloat16)
    grad_up_bias = jnp.sum(grad_pre.astype(jnp.float32), axis=(0, 1))
    grad_w_up = jnp.einsum(
        "snd,snf->df", saved_entry["normed_low"], grad_pre, preferred_element_type=jnp.float32
    )
    grad_normed = grad_resid_two + jnp.einsum(
        "snf,df->snd", grad_pre, w_up, preferred_element_type=jnp.float32
    )
    _, pull_one = jax.vjp(normalize, saved_entry["resid_one"], norm_gain[0], norm_shift[0])
    grad_resid_one, gain_one, shift_one = pull_one(grad_normed)
    attended_gradient = grad_resid_one.astype(jnp.bfloat16)
    grad_out_bias = jnp.sum(attended_gradient.astype(jnp.float32), axis=(0, 1))
    grad_w_out = jnp.einsum(
        "jhv,jhp->vp",
        saved_entry["context_low"],
        attended_gradient,
        preferred_element_type=jnp.float32,
    )
    grad_context = jnp.einsum(
        "yjo,io->yji", attended_gradient, output_weight, preferred_element_type=jnp.float32
    ).astype(jnp.bfloat16)
    grad_query, grad_key, grad_value = attend_back(
        saved_entry["queries"],
        saved_entry["key_rows"],
        saved_entry["value_rows"],
        lengths,
        head_count,
        grad_context,
        saved_entry["context"],
        saved_entry["log_total"],
    )
    grad_mixed = jnp.concatenate(
        [
            grad_query.astype(jnp.bfloat16),
            grad_key.astype(jnp.bfloat16),
            grad_value.astype(jnp.bfloat16),
        ],
        axis=-1,
    )
    grad_qv_bias = jnp.stack(
        [
            jnp.sum(grad_mixed[..., :model_width].astype(jnp.float32), axis=(0, 1)),
            jnp.sum(grad_mixed[..., 2 * model_width :].astype(jnp.float32), axis=(0, 1)),
        ]
    )
    grad_w_qkv = jnp.einsum(
        "snd,snf->df", saved_entry["rounded"], grad_mixed, preferred_element_type=jnp.float32
    )
    grad_current = grad_resid_one + jnp.einsum(
        "snf,df->snd", grad_mixed, w_qkv, preferred_element_type=jnp.float32
    )
    return (
        grad_current,
        (
            grad_w_qkv,
            grad_qv_bias,
            grad_w_out,
            grad_out_bias,
            grad_w_up,
            grad_up_bias,
            grad_w_down,
            grad_down_bias,
            jnp.stack([gain_one, gain_two]),
            jnp.stack([shift_one, shift_two]),
        ),
    )


def local(
    states,
    w_qkv,
    qv_bias,
    output_weight,
    out_bias,
    w_up,
    up_bias,
    w_down,
    down_bias,
    norm_gain,
    norm_shift,
    halt_weight,
    halt_bias,
    cotangent,
    lengths,
    caps,
):
    weights_tuple = (
        w_qkv,
        qv_bias,
        output_weight,
        out_bias,
        w_up,
        up_bias,
        w_down,
        down_bias,
        norm_gain,
        norm_shift,
    )
    head_count = HEADS
    current = states.astype(jnp.float32)
    inputs = []
    history = []
    prob_list = []
    for number in range(PONDER):
        if number < PONDER - 1:
            prob_list.append(jax.nn.sigmoid(jnp.sum(current * halt_weight, axis=-1) + halt_bias[0]))
        saved_entry = forward_block(current, weights_tuple, lengths, head_count)
        inputs.append(current)
        current = jnp.where((caps > number)[..., None], saved_entry["updated"], current)
        history.append(current)
    halt_probs = jnp.stack(prob_list, -1)
    (mixing, leftover), pull_halt = jax.vjp(lambda probs_in: halt_mix(probs_in, caps), halt_probs)
    final_state = jnp.zeros_like(current)
    for number in range(PONDER):
        final_state = final_state + mixing[..., number, None] * history[number]
    out_grad = cotangent.astype(jnp.float32)
    grad_mixing = jnp.stack(
        [jnp.sum(out_grad * history[number], axis=-1) for number in range(PONDER)], -1
    )
    grad_probs = pull_halt((grad_mixing, jnp.full(leftover.shape, PONDER_COST, jnp.float32)))[0]
    logits_gradient = grad_probs * halt_probs * (1.0 - halt_probs)
    totals = None
    grad_halt_weight = jnp.zeros(halt_weight.shape, jnp.float32)
    grad_halt_bias = jnp.zeros(halt_bias.shape, jnp.float32)
    grad_state = jnp.zeros(current.shape, jnp.float32)
    for number in reversed(range(PONDER)):
        grad_state = grad_state + out_grad * mixing[..., number, None]
        active = (caps > number)[..., None]
        grad_updated = jnp.where(active, grad_state, 0.0)
        passed = jnp.where(active, 0.0, grad_state)
        saved_entry = forward_block(inputs[number], weights_tuple, lengths, head_count)
        grad_prev, param_grads = backward_block(
            grad_updated, saved_entry, weights_tuple, lengths, head_count
        )
        totals = param_grads if totals is None else jax.tree.map(jnp.add, totals, param_grads)
        grad_state = passed + grad_prev
        if number < PONDER - 1:
            logit_grad = logits_gradient[..., number]
            grad_state = grad_state + logit_grad[..., None] * halt_weight
            grad_halt_weight = jnp.sum(logit_grad[..., None] * inputs[number], axis=(0, 1))
            grad_halt_bias = jnp.sum(logit_grad).reshape(1)
    summed = lax.psum(
        (
            totals[0],
            totals[1],
            totals[2],
            totals[3],
            totals[4],
            totals[5],
            totals[6],
            totals[7],
            totals[8],
            totals[9],
            grad_halt_weight,
            grad_halt_bias,
        ),
        ("dp", "seq"),
    )
    return (final_state, grad_state) + tuple(summed)


def solution(mesh):
    return jax.shard_map(
        local,
        mesh=mesh,
        in_specs=(
            P("dp", "seq", None),
            P(),
            P(),
            P(),
            P(),
            P(),
            P(),
            P(),
            P(),
            P(),
            P(),
            P(),
            P(),
            P("dp", "seq", None),
            P("dp"),
            P("dp", "seq"),
        ),
        out_specs=(
            P("dp", "seq", None),
            P("dp", "seq", None),
            P(),
            P(),
            P(),
            P(),
            P(),
            P(),
            P(),
            P(),
            P(),
            P(),
            P(),
            P(),
        ),
        check_vma=False,
    )
```

profile of v0, /device:TPU:1, one launch (start us, length us, event | category | flops | bytes accessed | tf_op | source)
XLA Modules:
  0.0 606.8 jit_solution(8028329383505341944)
XLA Ops:
  8.1 1.9 convolution_bitcast_fusion.4
  12.3 23.1 %all-gather.7.cloned.1.call-done = bf16[1,1024,512]{2,1,0:T(8,128)(2,1)} async-done(((bf16[1,128,512]{2,1,0:T(8,128)(2,1)}), bf16[1,1024,512]{2,1,0:T(8,128)(2,1)}) %all-gather.7.cloned.1.call-update) | async-done | bytes 1048592 | tf_op jit(solution)/shard_map/all_gather | solution.py:64
  35.4 1.5 copy.53
  36.9 22.4 %all-gather.5.cloned.1.call-done = bf16[1,1024,512]{2,1,0:T(8,128)(2,1)} async-done(((bf16[1,128,512]{2,1,0:T(8,128)(2,1)}), bf16[1,1024,512]{2,1,0:T(8,128)(2,1)}) %all-gather.5.cloned.1.call-update) | async-done | bytes 1048592 | tf_op jit(solution)/shard_map/all_gather | solution.py:63
  59.4 2.3 copy.52
  61.6 8.0 %while.86 = (s32[]{:T(128)}, f32[1,8,128]{2,1,0:T(8,128)S(1)}, f32[1,8,128]{2,1,0:T(8,128)S(1)}, f32[1,128,8,64]{1,3,2,0:T(8,128)}, s32[1]{0:T(128)}, /*index=5*...) while((s32[]{:T(128)}, f32[1,8,128]{2,1,0:T(8,128)S(1)}, ...), condition=%wide.region_4.5_spmd.clone, body=%wide.region_1.4_spmd.clone.sunk | while | flops 141237248 | bytes 12257531 | solution.py:94
  70.7 1.4 fusion.156
  72.8 2.1 convolution_add_fusion.4
  79.6 1.6 slice.94
  83.6 17.8 %all-gather.11.cloned.1.call-done = bf16[1,1024,512]{2,1,0:T(8,128)(2,1)} async-done(((bf16[1,128,512]{2,1,0:T(8,128)(2,1)}), bf16[1,1024,512]{2,1,0:T(8,128)(2,1)}) %all-gather.11.cloned.1.call-update) | async-done | bytes 1048592 | tf_op jit(solution)/shard_map/all_gather | solution.py:64
  101.4 2.3 copy.56
  103.7 21.5 %all-gather.9.cloned.1.call-done = bf16[1,1024,512]{2,1,0:T(8,128)(2,1)} async-done(((bf16[1,128,512]{2,1,0:T(8,128)(2,1)}), bf16[1,1024,512]{2,1,0:T(8,128)(2,1)}) %all-gather.9.cloned.1.call-update) | async-done | bytes 1048592 | tf_op jit(solution)/shard_map/all_gather | solution.py:63
  125.2 2.3 copy.55
  127.5 8.3 %while.87 = (s32[]{:T(128)}, f32[1,8,128]{2,1,0:T(8,128)S(1)}, f32[1,8,128]{2,1,0:T(8,128)S(1)}, f32[1,128,8,64]{1,3,2,0:T(8,128)}, s32[1]{0:T(128)}, /*index=5*...) while((s32[]{:T(128)}, f32[1,8,128]{2,1,0:T(8,128)S(1)}, ...), condition=%wide.region_12.13_spmd.clone, body=%wide.region_9.12_spmd.clone.sunk | while | flops 141237248 | bytes 12257531 | solution.py:94
  128.2 1.3 constant_dynamic-slice_fusion.15
  132.3 1.3 constant_dynamic-slice_fusion.15
  137.4 1.5 fusion.158
  139.1 2.1 convolution_add_fusion.3
  142.6 1.6 fusion.91
  145.1 1.7 convert_reduce_fusion.1
  146.8 1.5 multiply_reduce_fusion.2
  153.0 1.6 broadcast.630.clone.1
  154.5 1.6 broadcast.630.clone
  156.1 19.4 %while.88 = (s32[]{:T(128)}, f32[1,128,8,64]{1,3,2,0:T(8,128)}, f32[1,1024,512]{1,2,0:T(8,128)}, f32[1,1024,512]{1,2,0:T(8,128)}, bf16[1,1024,512]{1,2,0:T(8,128...) while((s32[]{:T(128)}, f32[1,128,8,64]{1,3,2,0:T(8,128)}, ...), condition=%wide.region_23.24_spmd.clone, body=%wide.region_22.23_spmd.clone.sunk | while | flops 339674112 | bytes 56108424 | solution.py:165
  177.7 30.3 %reduce-scatter.7.cloned.1.call-done = f32[1,128,512]{1,2,0:T(8,128)} async-done(((f32[1,1024,512]{1,2,0:T(8,128)}), f32[1,128,512]{1,2,0:T(8,128)}) %reduce-scatter.7.cloned.1.call-update) | async-done | bytes 262160 | tf_op jit(solution)/shard_map/reduce_scatter | solution.py:170
  208.0 2.2 convert_reduce_fusion.8
  210.2 35.1 %reduce-scatter.5.cloned.1.call-done = f32[1,128,512]{1,2,0:T(8,128)} async-done(((f32[1,1024,512]{1,2,0:T(8,128)}), f32[1,128,512]{1,2,0:T(8,128)}) %reduce-scatter.5.cloned.1.call-update) | async-done | bytes 262160 | tf_op jit(solution)/shard_map/reduce_scatter | solution.py:169
  246.3 3.2 multiply_reduce_fusion
  250.6 1.7 convert_reduce_fusion
  252.4 1.5 multiply_reduce_fusion.1
  255.3 1.6 broadcast.630.clone.2
  256.9 1.6 broadcast.630
  258.5 16.2 %while.89 = (s32[]{:T(128)}, f32[1,128,8,64]{1,3,2,0:T(8,128)S(1)}, f32[1,1024,512]{1,2,0:T(8,128)}, f32[1,1024,512]{1,2,0:T(8,128)}, bf16[1,1024,512]{1,2,0:T(8...) while((s32[]{:T(128)}, f32[1,128,8,64]{1,3,2,0:T(8,128)S(1)}, ...), condition=%wide.region_32.33_spmd.clone, body=%wide.region_31.32_spmd.clone.sunk | while | flops 339674112 | bytes 54011216 | solution.py:165
  276.0 1.5 fusion.145
  280.3 2.8 convolution_add_fusion.2
  283.1 2.8 convolution_add_fusion.1
  285.9 23.3 %reduce-scatter.11.cloned.1.call-done = f32[1,128,512]{1,2,0:T(8,128)} async-done(((f32[1,1024,512]{1,2,0:T(8,128)}), f32[1,128,512]{1,2,0:T(8,128)}) %reduce-scatter.11.cloned.1.call-update) | async-done | bytes 262160 | tf_op jit(solution)/shard_map/reduce_scatter | solution.py:170
  309.2 1.6 convert_reduce_fusion.6
  310.8 35.7 %reduce-scatter.9.cloned.1.call-done = f32[1,128,512]{1,2,0:T(8,128)} async-done(((f32[1,1024,512]{1,2,0:T(8,128)}), f32[1,128,512]{1,2,0:T(8,128)}) %reduce-scatter.9.cloned.1.call-update) | async-done | bytes 262160 | tf_op jit(solution)/shard_map/reduce_scatter | solution.py:169
  348.2 1.6 convolution_bitcast_fusion.2
  349.9 2.3 convolution_add_fusion
  353.9 43.6 %all-reduce = (f32[2,512]{1,0:T(2,128)}, f32[512]{0:T(512)}, f32[2048]{0:T(1024)}, f32[512]{0:T(512)}, f32[2,512]{1,0:T(2,128)}, /*index=5*/f32[2,512]{1,0:T(2,128)}, f32[512]{0:T(512)}, f32[1]{0:T(128)}) all-reduce(f32[2,512]{1,0:T(2,128)S(1)} %get-tuple-element.1094, ...), channel_id=1, replica_groups=mesh['dp'=4,'seq'=8] {'dp','seq'}, use_global_device_ids=true, to_apply=%region_42.43 | all-reduce | flops 6657 | bytes 53256 | tf_op jit(solution)/shard_map/psum | solution.py:396
  397.5 1.4 fusion.55
  398.9 189.7 %all-reduce.4.cloned.1.call-done = (f32[512,1536]{1,0:T(8,128)}, f32[512,512]{1,0:T(8,128)}, f32[512,2048]{1,0:T(8,128)}, f32[2048,512]{1,0:T(8,128)}) async-done(((f32[512,1536]{1,0:T(8,128)}, f32[512,512]{1,0:T(8,128)}, f32[512,2048]{1,0:T(8,128)}, f32[2048,512]{1,0:T(8,128)}), (f32[512,1536]{1,0:T(8,128)}, f32[512,512]{1,0:T(8,128)}, f32[512,2048]{1,0:T(8,128)}, ...) | async-done | bytes 12582928 | tf_op jit(solution)/shard_map/psum | solution.py:396
  588.6 3.9 copy.124
  593.5 2.1 copy.126
  595.6 1.6 copy-done.30
  597.2 2.1 copy.127
  (484 shorter events, 82.5 us)
Async XLA Ops:
  7.2 67.7 %copy-start = (bf16[2048,512]{1,0:T(8,128)(2,1)S(1)}, bf16[2048,512]{1,0:T(8,128)(2,1)}, u32[]{:S(2)}) copy-start(bf16[2048,512]{1,0:T(8,128)(2,1)} %param.31) | copy-start | bytes 6291460
  7.2 4.5 copy-start.126
  7.2 5.0 copy-start.118
  7.2 5.0 copy-start.119
  7.2 28.2 %all-gather.7.cloned.1.call-start = ((), (), s32[]{:S(2)}) async-start(), calls=%async_computation.5 | async-start | bytes 1179648 | tf_op jit(solution)/shard_map/all_gather | solution.py:64
  10.7 48.7 %all-gather.5.cloned.1.call-start = ((), (), s32[]{:S(2)}) async-start(), calls=%async_computation.4 | async-start | bytes 1179648 | tf_op jit(solution)/shard_map/all_gather | solution.py:63
  11.5 90.0 %all-gather.11.cloned.1.call-start = ((), (), s32[]{:S(2)}) async-start(), calls=%async_computation.7 | async-start | bytes 1179648 | tf_op jit(solution)/shard_map/all_gather | solution.py:64
  12.2 63.9 %copy-start.133 = (pred[128]{0:T(512)(128)(4,1)}, pred[128]{0:T(512)(128)(4,1)S(1)}, u32[]{:S(2)}) copy-start(pred[128]{0:T(512)(128)(4,1)S(1)} %get-tuple-element.1078) | copy-start | bytes 388
  12.2 62.6 %copy-start.75 = (f32[1,512]{1,0:T(1,128)}, f32[1,512]{1,0:T(1,128)S(1)}, u32[]{:S(2)}) copy-start(f32[1,512]{1,0:T(1,128)S(1)} %get-tuple-element.1072) | copy-start | bytes 6148
  12.3 63.9 %copy-start.81 = (f32[1,512]{1,0:T(1,128)}, f32[1,512]{1,0:T(1,128)S(1)}, u32[]{:S(2)}) copy-start(f32[1,512]{1,0:T(1,128)S(1)} %get-tuple-element.1071) | copy-start | bytes 6148
  12.3 62.6 %copy-start.78 = (f32[1,512]{1,0:T(1,128)}, f32[1,512]{1,0:T(1,128)S(1)}, u32[]{:S(2)}) copy-start(f32[1,512]{1,0:T(1,128)S(1)} %get-tuple-element.1074) | copy-start | bytes 6148
  12.3 63.8 %copy-start.88 = (f32[1,512]{1,0:T(1,128)}, f32[1,512]{1,0:T(1,128)S(1)}, u32[]{:S(2)}) copy-start(f32[1,512]{1,0:T(1,128)S(1)} %get-tuple-element.1073) | copy-start | bytes 6148
  61.6 9.0 %copy-start.34 = (bf16[1,128,512]{2,1,0:T(8,128)(2,1)S(1)}, bf16[1,128,512]{2,1,0:T(8,128)(2,1)}, u32[]{:S(2)}) copy-start(bf16[1,128,512]{2,1,0:T(8,128)(2,1)} %param.24) | copy-start | bytes 393220
  61.6 9.0 %copy-start.95 = (f32[512]{0:T(512)S(1)}, f32[512]{0:T(512)}, u32[]{:S(2)}) copy-start(f32[512]{0:T(512)} %param.28) | copy-start | bytes 6148
  61.6 11.2 %copy-start.84 = (f32[2048]{0:T(1024)S(1)}, f32[2048]{0:T(1024)}, u32[]{:S(2)}) copy-start(f32[2048]{0:T(1024)} %param.30) | copy-start | bytes 24580
  79.5 45.7 %all-gather.9.cloned.1.call-start = ((), (), s32[]{:S(2)}) async-start(), calls=%async_computation.6 | async-start | bytes 1179648 | tf_op jit(solution)/shard_map/all_gather | solution.py:63
  81.2 126.8 %reduce-scatter.7.cloned.1.call-start = ((), (), s32[]{:S(2)}) async-start(), calls=%async_computation.9 | async-start | bytes 2359296 | tf_op jit(solution)/shard_map/reduce_scatter | solution.py:170
  83.0 44.5 %copy-start.128 = (f32[128]{0:T(128)}, f32[128]{0:T(128)S(1)}, u32[]{:S(2)}) copy-start(f32[128]{0:T(128)S(1)} %get-tuple-element.1051) | copy-start | bytes 1540
  83.0 59.2 %copy-start.122 = (f32[128]{0:T(128)}, f32[128]{0:T(128)S(1)}, u32[]{:S(2)}) copy-start(f32[128]{0:T(128)S(1)} %get-tuple-element.1050) | copy-start | bytes 1540
  83.6 60.5 %copy-start.121 = (f32[128]{0:T(128)}, f32[128]{0:T(128)S(1)}, u32[]{:S(2)}) copy-start(f32[128]{0:T(128)S(1)} %fusion.125) | copy-start | bytes 1540
  127.5 9.9 %copy-start.96 = (f32[512]{0:T(512)S(1)}, f32[512]{0:T(512)}, u32[]{:S(2)}) copy-start(f32[512]{0:T(512)} %param.28) | copy-start | bytes 6148
  127.5 11.6 %copy-start.76 = (f32[1,512]{1,0:T(1,128)S(1)}, f32[1,512]{1,0:T(1,128)}, u32[]{:S(2)}) copy-start(f32[1,512]{1,0:T(1,128)} %copy-done.75) | copy-start | bytes 6148
  127.5 11.6 %copy-start.79 = (f32[1,512]{1,0:T(1,128)S(1)}, f32[1,512]{1,0:T(1,128)}, u32[]{:S(2)}) copy-start(f32[1,512]{1,0:T(1,128)} %copy-done.78) | copy-start | bytes 6148
  127.5 11.6 %copy-start.85 = (f32[2048]{0:T(1024)S(1)}, f32[2048]{0:T(1024)}, u32[]{:S(2)}) copy-start(f32[2048]{0:T(1024)} %param.30) | copy-start | bytes 24580
  138.9 9.5 %copy-start.10 = (f32[1,128,512]{2,1,0:T(8,128)}, f32[1,128,512]{2,1,0:T(8,128)S(1)}, u32[]{:S(2)}) copy-start(f32[1,128,512]{2,1,0:T(8,128)S(1)} %get-tuple-element.1084) | copy-start | bytes 786436
  138.9 9.4 %copy-start.93 = (f32[128]{0:T(128)}, f32[128]{0:T(128)S(1)}, u32[]{:S(2)}) copy-start(f32[128]{0:T(128)S(1)} %broadcast_multiply_fusion.1) | copy-start | bytes 1540
  139.1 9.2 %copy-start.113 = (f32[128]{0:T(128)}, f32[128]{0:T(128)S(1)}, u32[]{:S(2)}) copy-start(f32[128]{0:T(128)S(1)} %fusion.137) | copy-start | bytes 1540
  175.6 70.7 %copy-start.83 = (f32[1,512]{1,0:T(1,128)S(1)}, f32[1,512]{1,0:T(1,128)}, u32[]{:S(2)}) copy-start(f32[1,512]{1,0:T(1,128)} %copy-done.81) | copy-start | bytes 6148
  175.6 69.7 %reduce-scatter.5.cloned.1.call-start = ((), (), s32[]{:S(2)}) async-start(), calls=%async_computation.8 | async-start | bytes 2359296 | tf_op jit(solution)/shard_map/reduce_scatter | solution.py:169
  176.2 133.0 %reduce-scatter.11.cloned.1.call-start = ((), (), s32[]{:S(2)}) async-start(), calls=%async_computation.11 | async-start | bytes 2359296 | tf_op jit(solution)/shard_map/reduce_scatter | solution.py:170
  210.2 39.3 %copy-start.38 = (f32[1,128,512]{2,1,0:T(8,128)S(1)}, f32[1,128,512]{2,1,0:T(8,128)}, u32[]{:S(2)}) copy-start(f32[1,128,512]{2,1,0:T(8,128)} %copy-done.37) | copy-start | bytes 786436
  210.2 39.3 %copy-start.115 = (f32[128]{0:T(128)S(1)}, f32[128]{0:T(128)}, u32[]{:S(2)}) copy-start(f32[128]{0:T(128)} %copy-done.114) | copy-start | bytes 1540
  245.3 4.2 copy-start.137
  254.1 4.4 copy-start.51
  274.7 71.8 %reduce-scatter.9.cloned.1.call-start = ((), (), s32[]{:S(2)}) async-start(), calls=%async_computation.10 | async-start | bytes 2359296 | tf_op jit(solution)/shard_map/reduce_scatter | solution.py:169
  275.5 313.1 %all-reduce.4.cloned.1.call-start = ((), (), s32[]{:S(2)}) async-start(), calls=%async_computation.12 | async-start | bytes 25165824 | tf_op jit(solution)/shard_map/psum | solution.py:396
  283.1 65.1 %copy-start.35 = (bf16[1,128,512]{2,1,0:T(8,128)(2,1)S(1)}, bf16[1,128,512]{2,1,0:T(8,128)(2,1)}, u32[]{:S(2)}) copy-start(bf16[1,128,512]{2,1,0:T(8,128)(2,1)} %param.24) | copy-start | bytes 393220
  310.8 39.0 %copy-start.24 = (f32[1,128,512]{2,1,0:T(8,128)S(1)}, f32[1,128,512]{2,1,0:T(8,128)}, u32[]{:S(2)}) copy-start(f32[1,128,512]{2,1,0:T(8,128)} %copy-done.22) | copy-start | bytes 786436
  352.3 45.1 %copy-start.26 = (bf16[512,1536]{1,0:T(8,128)(2,1)S(1)}, bf16[512,1536]{1,0:T(8,128)(2,1)}, u32[]{:S(2)}) copy-start(bf16[512,1536]{1,0:T(8,128)(2,1)} %param.25) | copy-start | bytes 4718596
  352.3 45.1 %copy-start.52 = (f32[1,128,512]{2,1,0:T(8,128)S(1)}, f32[1,128,512]{2,1,0:T(8,128)}, u32[]{:S(2)}) copy-start(f32[1,128,512]{2,1,0:T(8,128)} %copy-done.51) | copy-start | bytes 786436
  352.3 45.1 %copy-start.67 = (bf16[1,128,8,64]{1,3,2,0:T(8,128)(2,1)S(1)}, bf16[1,128,8,64]{1,3,2,0:T(8,128)(2,1)}, u32[]{:S(2)}) copy-start(bf16[1,128,8,64]{1,3,2,0:T(8,128)(2,1)} %get-tuple-element.1035) | copy-start | bytes 393220
  352.3 45.1 %copy-start.68 = (bf16[1,128,512]{1,2,0:T(8,128)(2,1)S(1)}, bf16[1,128,512]{1,2,0:T(8,128)(2,1)}, u32[]{:S(2)}) copy-start(bf16[1,128,512]{1,2,0:T(8,128)(2,1)} %get-tuple-element.1037) | copy-start | bytes 393220
  352.4 45.1 %copy-start.70 = (bf16[1,128,512]{1,2,0:T(8,128)(2,1)S(1)}, bf16[1,128,512]{1,2,0:T(8,128)(2,1)}, u32[]{:S(2)}) copy-start(bf16[1,128,512]{1,2,0:T(8,128)(2,1)} %copy-done.69) | copy-start | bytes 393220
  352.4 45.1 %copy-start.74 = (f32[1,128,512]{2,1,0:T(8,128)S(1)}, f32[1,128,512]{2,1,0:T(8,128)}, u32[]{:S(2)}) copy-start(f32[1,128,512]{2,1,0:T(8,128)} %copy-done.73) | copy-start | bytes 786436
  352.4 45.1 %copy-start.132 = (f32[512]{0:T(512)S(1)}, f32[512]{0:T(512)}, u32[]{:S(2)}) copy-start(f32[512]{0:T(512)} %param.35) | copy-start | bytes 6148
  352.4 45.1 %copy-start.135 = (pred[128]{0:T(512)(128)(4,1)S(1)}, pred[128]{0:T(512)(128)(4,1)}, u32[]{:S(2)}) copy-start(pred[128]{0:T(512)(128)(4,1)} %copy-done.133) | copy-start | bytes 388
  352.4 45.1 %copy-start.143 = (f32[128]{0:T(128)S(1)}, f32[128]{0:T(128)}, u32[]{:S(2)}) copy-start(f32[128]{0:T(128)} %copy-done.142) | copy-start | bytes 1540
  588.6 4.9 copy-start.31
  (122 other events, 231.3 us)
Sparse Core Ops, SparseCore 0:
  10.8 24.5 all-gather.6
  37.6 21.7 all-gather.4
  79.7 21.7 all-gather.10
  103.5 21.7 all-gather.8
  175.7 32.2 reduce-scatter.6
  210.7 34.5 reduce-scatter.4
  274.8 34.3 reduce-scatter.10
  312.1 34.4 reduce-scatter.8
  354.1 234.3 all-reduce.3
where the time goes:
time: 609 us; the launch traced here: 607 us
  waiting for transfers between devices  400 us (66%)
  local copies, waits for them, and re-layouts  63.5 us (10%)
  matrix products  51.9 us (9%)
  blocking collectives  43.6 us (7%)
  other arithmetic  29.8 us (5%)
  between operations  16.1 us (3%)
    psum x1, waiting for transfers between devices, local(): lax.psum((totals[0], totals[1], totals[2], totals[3], totals[4], totals[5...  190 us
    reduce_scatter x2, waiting for transfers between devices, attend_back(): lax.psum_scatter(grad_key_all, 'seq', scatter_dimension=1, tiled=True)  70.8 us
    reduce_scatter x2, waiting for transfers between devices, attend_back(): lax.psum_scatter(grad_value_all, 'seq', scatter_dimension=1, tiled=True)  53.6 us
    all_gather x2, waiting for transfers between devices, attend(): key_piece = lax.all_gather(key_rows, 'seq', axis=1, tiled=True)  44 us
    psum x1, blocking collectives, local(): lax.psum((totals[0], totals[1], totals[2], totals[3], totals[4], totals[5...  43.6 us
    all_gather x2, waiting for transfers between devices, attend(): value_piece = lax.all_gather(value_rows, 'seq', axis=1, tiled=True)  40.9 us
    unnamed x274, local copies, waits for them, and re-layouts  25 us
    while x60, local copies, waits for them, and re-layouts  14.9 us
  transfers between devices with their start and end apart: 9, of which 9 were waited for; matrix products, arithmetic and copies ran while one was open for 4% of the time, Pallas kernels for 0%

commit v1 on v0

--- a/solution.py
+++ b/solution.py
@@ -3,6 +3,8 @@
 import jax
 import jax.numpy as jnp
 from jax import lax
+from jax.experimental import pallas as pl
+from jax.experimental.pallas import tpu as pltpu
 from jax.sharding import PartitionSpec as P
 
 HEADS = 8
@@ -413,43 +415,675 @@
     return (final_state, grad_state) + tuple(summed)
 
 
+BF = jnp.bfloat16
+F32 = jnp.float32
+MESH = pl.DeviceIdType.MESH
+GELU_A = math.sqrt(2.0 / math.pi)
+GELU_B = 0.044715
+
+
+def nn(a, b):
+    return lax.dot_general(a, b, (((1,), (0,)), ((), ())), preferred_element_type=F32)
+
+
+def nt(a, b):
+    return lax.dot_general(a, b, (((1,), (1,)), ((), ())), preferred_element_type=F32)
+
+
+def tn(a, b):
+    return lax.dot_general(a, b, (((0,), (0,)), ((), ())), preferred_element_type=F32)
+
+
+def colsum(v):
+    return jnp.sum(v, axis=0, keepdims=True)
+
+
+def rowsum(v):
+    return jnp.sum(v, axis=1, keepdims=True)
+
+
+class Links:
+    def __init__(self, send, recv):
+        self.send, self.recv, self.used, self.open = send, recv, 0, []
+
+    def copy(self, src, dst, device):
+        at = self.used
+        self.used += 1
+        made = pltpu.make_async_remote_copy(
+            src_ref=src,
+            dst_ref=dst,
+            send_sem=self.send.at[at],
+            recv_sem=self.recv.at[at],
+            device_id=device,
+            device_id_type=MESH,
+        )
+        return made
+
+    def start(self, src, dst, device):
+        made = self.copy(src, dst, device)
+        made.start()
+        self.open.append(made)
+        return made
+
+    def drain(self):
+        for made in self.open:
+            made.wait_send()
+        self.open = []
+
+
+N_LINKS = 160
+TOK = 128
+ROWS = 256
+WIDE = 512
+HALF = 1024
+FEAT = 256
+HEADC = 4
+KEYS = 256
+SLOTS = 4
+QROWS = HEADC * ROWS
+CHUNK = 128
+
+
+def fused_kernel(
+    states, cot_in, aux_in, vec, wqkv_all, wout_all, wup_all, wdown_all,
+    final_out, igrad_out, small_out, gqkv_out, gout_out, gup_out, gdown_out,
+    send_sem, recv_sem, local_sem,
+    wqkv, wout, wup, wdown,
+    st, ct, ax,
+    s, rnd, q4, kv, ctxt, ctxlt, x1, rs1, n1low, hid, dgelu, x2, rs2, logt,
+    scores, dprobs, probs, dsc, mrow, lrow, part_ctx, drow, do4,
+    xch, xrecv, gcur, gres, dqt, dkv_own, dkv_send, dkv_recv, dqkv, small,
+    gdown, gup, gqkv, gout,
+    sa_all, ra_all, sb_all, rb_all, sc_all, rc_all, u_all, out_all,
+    smallx, fin_t, ig_t,
+):
+    dp = lax.axis_index("dp")
+    sq = lax.axis_index("seq")
+    x, y = lax.rem(dp, 2), dp // 2
+    z, c = sq // 2, lax.rem(sq, 2)
+
+    def flip(value, bit):
+        return value + bit - 2 * bit * lax.rem(value // bit, 2)
+
+    sib = (dp, flip(sq, 1))
+    to_x = (flip(dp, 1), sq)
+    to_y = (flip(dp, 2), sq)
+    z1 = (dp, flip(sq, 2))
+    z2 = (dp, flip(sq, 4))
+    z3 = (dp, flip(flip(sq, 2), 4))
+    diag = (flip(dp, 1), flip(sq, 2))
+    swap = (flip(dp, 1), flip(sq, 4))
+    peers = (sib, to_x, to_y, z1, z2, z3, diag, swap)
+
+    loads = []
+
+    def load(src, dst):
+        made = pltpu.make_async_copy(src, dst, local_sem.at[len(loads)])
+        made.start()
+        loads.append(made)
+
+    own = pl.multiple_of(c * FEAT, FEAT)
+    for third in range(3):
+        load(
+            wqkv_all.at[:, pl.ds(pl.multiple_of(third * WIDE + own, FEAT), FEAT)],
+            wqkv.at[:, pl.ds(third * FEAT, FEAT)],
+        )
+    load(wout_all.at[pl.ds(own, FEAT), :], wout)
+    wide_own = pl.multiple_of(c * HALF, HALF)
+    load(wup_all.at[:, pl.ds(wide_own, HALF)], wup)
+    load(wdown_all.at[pl.ds(wide_own, HALF), :], wdown)
+
+    barrier = pltpu.get_barrier_semaphore()
+    for peer in peers:
+        pl.semaphore_signal(barrier, inc=1, device_id=peer, device_id_type=MESH)
+    pl.semaphore_wait(barrier, len(peers))
+
+    links = Links(send_sem, recv_sem)
+
+    moved = x != z // 2
+    swaps = [
+        links.copy(states, st.at[c], swap),
+        links.copy(aux_in, ax.at[c], swap),
+        links.copy(cot_in, ct.at[c], swap),
+    ]
+
+    @pl.when(moved)
+    def _():
+        for made in swaps:
+            made.start()
+        swaps[0].wait_recv()
+        swaps[1].wait_recv()
+
+    @pl.when(jnp.logical_not(moved))
+    def _():
+        st[c] = states[...]
+        ax[c] = aux_in[...]
+        ct[c] = cot_in[...]
+
+    pair_st = links.start(st.at[c], st.at[c], sib)
+    pair_ax = links.start(ax.at[c], ax.at[c], sib)
+    pair_st.wait_recv()
+    pair_ax.wait_recv()
+
+    caps = ax[...].reshape(ROWS, 128)[:, 0:1]
+    length = ax[0, 0:1, 1:2]
+    def block_of(xx, zz):
+        return jnp.where(xx == zz // 2, zz, flip(zz, 2))
+
+    zf, xf = flip(z, 1), 1 - x
+    places = (block_of(x, z), block_of(xf, z), block_of(x, zf), block_of(xf, zf))
+    key_iota = lax.broadcasted_iota(jnp.int32, (KEYS, 1), 0)
+    biases = []
+    for place in places:
+        positions = (key_iota + place * KEYS).astype(F32)
+        biases.append(jnp.where(positions < length, 0.0, MASK_FILL))
+
+    row = lambda i: vec[i : i + 1, :]
+    mine = lambda v: jnp.where(c == 0, v[:, :FEAT], v[:, FEAT:])
+    bias_q, bias_v = mine(row(0)), mine(row(1))
+    up_bias = jnp.concatenate(
+        [jnp.where(c == 0, row(3), row(5)), jnp.where(c == 0, row(4), row(6))], axis=1
+    )
+    lane_head = lax.broadcasted_iota(jnp.int32, (1, FEAT), 1) // 64
+
+    s[0] = st[...].reshape(ROWS, WIDE).astype(F32)
+    small[...] = jnp.zeros_like(small)
+    for made in loads:
+        made.wait()
+
+    def exchange(value, at):
+        xch[at] = value
+        made = links.start(xch.at[at], xrecv.at[at], sib)
+        made.wait_recv()
+
+    def norm(resid):
+        centered = resid - jnp.mean(resid, axis=1, keepdims=True)
+        scale = lax.rsqrt(jnp.mean(centered * centered, axis=1, keepdims=True) + NORM_EPSILON)
+        return centered * scale, scale
+
+    BAND = 64
+
+    def bands(body):
+        for at in range(0, ROWS, BAND):
+            body(slice(at, at + BAND))
+
+    def forward(n):
+        rounded = s[n].astype(BF)
+        rnd[n] = rounded
+        kv[n, 0, :, :FEAT] = nn(rounded, wqkv[:, FEAT : 2 * FEAT]).astype(BF)
+        kv[n, 0, :, FEAT:] = (nn(rounded, wqkv[:, 2 * FEAT :]) + bias_v).astype(BF)
+        came = [None]
+        for slot, peer in ((1, to_x), (2, z1), (3, diag)):
+            came.append(links.start(kv.at[n, 0], kv.at[n, slot], peer))
+        q = (nn(rounded, wqkv[:, :FEAT]) + bias_q).astype(BF)
+        qs = (q.astype(F32) * 0.125).astype(BF)
+        for h in range(HEADC):
+            q4[n, h * ROWS : (h + 1) * ROWS, :] = jnp.where(lane_head == h, qs, jnp.zeros_like(qs))
+        for slot in range(SLOTS):
+            if slot:
+                came[slot].wait_recv()
+            scores[...] = nt(kv[n, slot, :, :FEAT], q4[n])
+            for at in range(0, QROWS, CHUNK):
+                cut = slice(at, at + CHUNK)
+                part = scores[:, cut] + biases[slot]
+                top = jnp.max(part, axis=0, keepdims=True)
+                e = jnp.exp(part - top)
+                mrow[slot : slot + 1, cut] = top
+                lrow[slot : slot + 1, cut] = colsum(e)
+                probs[:, cut] = e.astype(BF)
+            vt = kv[n, slot, :, FEAT:].T
+            for h in range(HEADC):
+                part_ctx[slot, h * 64 : (h + 1) * 64, :] = nn(
+                    vt[h * 64 : (h + 1) * 64, :], probs[:, h * ROWS : (h + 1) * ROWS]
+                )
+        top = jnp.max(mrow[...], axis=0, keepdims=True)
+        weight = jnp.exp(mrow[...] - top)
+        total = jnp.sum(weight * lrow[...], axis=0, keepdims=True)
+        logt[n] = top + jnp.log(total)
+        weight = weight / total
+        for h in range(HEADC):
+            hr, hc = slice(h * 64, (h + 1) * 64), slice(h * ROWS, (h + 1) * ROWS)
+            acc = part_ctx[0, hr, :] * weight[0:1, hc]
+            for slot in range(1, SLOTS):
+                acc = acc + part_ctx[slot, hr, :] * weight[slot : slot + 1, hc]
+            ctxt[n, hr, :] = acc
+        low = ctxt[n].astype(BF)
+        ctxlt[n] = low
+        exchange(tn(low, wout[...]), 2 * n)
+
+        def first(band):
+            resid = s[n, band, :] + (xch[2 * n, band, :] + xrecv[2 * n, band, :]) + row(2)
+            hat, scale = norm(resid)
+            x1[n, band, :] = hat
+            rs1[n, band, :] = scale
+            normed = hat * row(8) + row(10)
+            gres[band, :] = normed
+            n1low[n, band, :] = normed.astype(BF)
+
+        bands(first)
+        scores[...] = nn(n1low[n], wup[...]) + up_bias
+
+        def act(band):
+            v = scores[band, :]
+            sq_v = v * v
+            t = jnp.tanh(GELU_A * v * (1.0 + GELU_B * sq_v))
+            half = 0.5 * (1.0 + t)
+            hid[n, band, :] = (v * half).astype(BF)
+            dgelu[n, band, :] = half + (0.5 * GELU_A) * v * (1.0 - t * t) * (
+                1.0 + (3.0 * GELU_B) * sq_v
+            )
+
+        bands(act)
+        exchange(nn(hid[n], wdown[...]), 2 * n + 1)
+
+        def second(band):
+            at = 2 * n + 1
+            resid = gres[band, :] + (xch[at, band, :] + xrecv[at, band, :]) + row(7)
+            hat, scale = norm(resid)
+            x2[n, band, :] = hat
+            rs2[n, band, :] = scale
+            updated = hat * row(9) + row(11)
+            s[n + 1, band, :] = jnp.where(caps[band, :] > n, updated, s[n, band, :])
+
+        bands(second)
+
+    for n in range(PONDER):
+        forward(n)
+
+    @pl.when(moved)
+    def _():
+        swaps[2].wait_recv()
+
+    pair_ct = links.start(ct.at[c], ct.at[c], sib)
+    pair_ct.wait_recv()
+    halt = jax.nn.sigmoid(rowsum(s[0] * row(12)) + vec[13:14, 0:1])
+    more = caps > 1.0
+    mix_one = jnp.where(more, halt, 1.0)
+    mix_two = jnp.where(more, 1.0 - halt, 0.0)
+    fin_t[...] = mix_one * s[1] + mix_two * s[2]
+    mine_rows = pl.ds(pl.multiple_of(c * TOK, TOK), TOK)
+    fin_copy = links.copy(fin_t.at[mine_rows, :], final_out, swap)
+
+    @pl.when(moved)
+    def _():
+        fin_copy.start()
+
+    @pl.when(jnp.logical_not(moved))
+    def _():
+        final_out[...] = fin_t[mine_rows, :]
+
+    cot = ct[...].reshape(ROWS, WIDE).astype(F32)
+    grad_halt = jnp.where(
+        more, rowsum(cot * s[1]) - rowsum(cot * s[2]) - PONDER_COST, 0.0
+    )
+    grad_logit = grad_halt * halt * (1.0 - halt)
+    small[9:10, :] = colsum(grad_logit * s[0])
+    small[10:11, :] = jnp.broadcast_to(colsum(grad_logit), (1, WIDE))
+
+    def norm_back(grad, hat, scale, gain):
+        g = grad * gain
+        a = jnp.mean(g, axis=1, keepdims=True)
+        b = jnp.mean(g * hat, axis=1, keepdims=True)
+        return scale * (g - a - hat * b)
+
+    def add_small(at, value):
+        small[at : at + 1, : value.shape[1]] += value
+
+    def add_grad(ref, value, first_time):
+        value = value.reshape(ref.shape)
+        if first_time:
+            ref[...] = value
+        else:
+            ref[...] += value
+
+    def backward(n, last):
+        def two(band):
+            active = caps[band, :] > n
+            grad = jnp.where(active, gcur[band, :], 0.0)
+            hat = x2[n, band, :]
+            back = norm_back(grad, hat, rs2[n, band, :], row(9))
+            gres[band, :] = back
+            add_small(6, colsum(grad * hat))
+            add_small(8, colsum(grad))
+            rounded = back.astype(BF)
+            add_small(4, colsum(rounded.astype(F32)))
+            gmlp[band, :] = rounded
+            gcur[band, :] = jnp.where(active, 0.0, gcur[band, :])
+
+        gmlp = n1low.at[PONDER]
+        bands(two)
+        add_grad(gdown, tn(hid[n], gmlp[...]), last)
+        scores[...] = nt(gmlp[...], wdown[...])
+
+        def pre(band):
+            grad = (dgelu[n, band, :] * scores[band, :]).astype(BF)
+            probs[band, :] = grad
+            total = colsum(grad.astype(F32))
+            add_small(2, total[:, :WIDE])
+            add_small(3, total[:, WIDE:])
+
+        bands(pre)
+        add_grad(gup, tn(n1low[n], probs[...]), last)
+        at = 2 * PONDER + 2 * n
+        exchange(nt(probs[...], wup[...]), at)
+
+        def one(band):
+            grad = gres[band, :] + (xch[at, band, :] + xrecv[at, band, :])
+            hat = x1[n, band, :]
+            back = norm_back(grad, hat, rs1[n, band, :], row(8))
+            gres[band, :] = back
+            add_small(5, colsum(grad * hat))
+            add_small(7, colsum(grad))
+            rounded = back.astype(BF)
+            add_small(1, colsum(rounded.astype(F32)))
+            gmlp[band, :] = rounded
+
+        bands(one)
+        add_grad(gout, nn(ctxlt[n], gmlp[...]), last)
+        gctx = nt(gmlp[...], wout[...]).astype(BF)
+        for h in range(HEADC):
+            do4[h * ROWS : (h + 1) * ROWS, :] = jnp.where(lane_head == h, gctx, jnp.zeros_like(gctx))
+        dots = nt(wout[...], gmlp[...]).astype(BF).astype(F32) * ctxt[n]
+        for h in range(HEADC):
+            drow[:, h * ROWS : (h + 1) * ROWS] = colsum(dots[h * 64 : (h + 1) * 64, :])
+        came = [None] * SLOTS
+        order = (3, 1, 2, 0)
+        to = (None, to_x, z1, diag)
+        for number, slot in enumerate(order):
+            scores[...] = nt(kv[n, slot, :, :FEAT], q4[n])
+            dprobs[...] = nt(kv[n, slot, :, FEAT:], do4[...])
+            for cut_at in range(0, QROWS, CHUNK):
+                cut = slice(cut_at, cut_at + CHUNK)
+                p = jnp.exp(scores[:, cut] + biases[slot] - logt[n, :, cut])
+                probs[:, cut] = p.astype(BF)
+                dsc[:, cut] = (p * (dprobs[:, cut] - drow[:, cut])).astype(BF)
+            dk = nn(dsc[...], q4[n])
+            dv = nn(probs[...], do4[...])
+            if slot:
+                dkv_send[n, slot - 1, :, :FEAT] = dk.astype(BF)
+                dkv_send[n, slot - 1, :, FEAT:] = dv.astype(BF)
+                came[slot] = links.start(
+                    dkv_send.at[n, slot - 1], dkv_recv.at[n, slot - 1], to[slot]
+                )
+            else:
+                dkv_own[:, :FEAT] = dk
+                dkv_own[:, FEAT:] = dv
+            kt = kv[n, slot, :, :FEAT].T
+            for h in range(HEADC):
+                hr = slice(h * 64, (h + 1) * 64)
+                term = nn(kt[hr, :], dsc[:, h * ROWS : (h + 1) * ROWS])
+                if number == 0:
+                    dqt[hr, :] = term
+                else:
+                    dqt[hr, :] += term
+        dqkv[:, :FEAT] = (dqt[...] * 0.125).T.astype(BF)
+        for slot in range(1, SLOTS):
+            came[slot].wait_recv()
+        dqkv[:, FEAT:] = (
+            dkv_own[...]
+            + dkv_recv[n, 0].astype(F32)
+            + dkv_recv[n, 1].astype(F32)
+            + dkv_recv[n, 2].astype(F32)
+        ).astype(BF)
+        add_small(0, jnp.concatenate(
+            [colsum(dqkv[:, :FEAT].astype(F32)), colsum(dqkv[:, 2 * FEAT :].astype(F32))], axis=1
+        ))
+        at = 2 * PONDER + 2 * n + 1
+        exchange(nt(dqkv[...], wqkv[...]), at)
+        add_grad(gqkv, tn(rnd[n], dqkv[...]), last)
+
+        def prev(band):
+            gcur[band, :] = gcur[band, :] + gres[band, :] + (xch[at, band, :] + xrecv[at, band, :])
+
+        bands(prev)
+
+    gcur[...] = cot * mix_two
+    backward(1, True)
+    gcur[...] = gcur[...] + cot * mix_one
+    backward(0, False)
+    ig_t[...] = gcur[...] + grad_logit * row(12)
+    ig_copy = links.copy(ig_t.at[mine_rows, :], igrad_out, swap)
+
+    @pl.when(moved)
+    def _():
+        ig_copy.start()
+
+    @pl.when(jnp.logical_not(moved))
+    def _():
+        igrad_out[...] = ig_t[mine_rows, :]
+
+    grads = (gup, gdown, gqkv, gout)
+    jobs = []
+    for at, ref in enumerate(grads):
+        quarter, width = ref.shape[2], ref.shape[3]
+        jobs.append((ref, quarter, width, width // 2, sa_all[at], ra_all[at], sb_all[at], rb_all[at],
+                     sc_all[at], rc_all[at], u_all[at], out_all[at]))
+    stage_one, stage_two, stage_three = [], [], []
+    small_one = links.start(small, smallx.at[0], to_x)
+    for ref, quarter, width, half, sa, ra, sb, rb, sc, rc, u, out in jobs:
+        sa[0] = ref[1 - x, :, :, :half].astype(BF)
+        sa[1] = ref[:, 1 - y, :, half:].astype(BF)
+        stage_one.append((links.start(sa.at[0], ra.at[0], to_x), links.start(sa.at[1], ra.at[1], to_y)))
+    small_one.wait_recv()
+    smallx[1] = small[...] + smallx[0]
+    small_two = links.start(smallx.at[1], smallx.at[2], to_y)
+    for (ref, quarter, width, half, sa, ra, sb, rb, sc, rc, u, out), (ca, cb) in zip(jobs, stage_one):
+        ca.wait_recv()
+        sb[0] = (ref[x, 1 - y, :, :half] + ra[0, 1 - y].astype(F32)).astype(BF)
+        cb.wait_recv()
+        sb[1] = (ref[1 - x, y, :, half:] + ra[1, 1 - x].astype(F32)).astype(BF)
+        stage_two.append((links.start(sb.at[0], rb.at[0], to_y), links.start(sb.at[1], rb.at[1], to_x)))
+    small_two.wait_recv()
+    smallx[3] = smallx[1] + smallx[2]
+    smallx[4 + z] = smallx[3]
+    zs = (z1, z2, z3)
+    small_three = [links.start(smallx.at[3], smallx.at[4 + z], peer) for peer in zs]
+    zpos = (flip(z, 1), flip(z, 2), flip(flip(z, 1), 2))
+    for (ref, quarter, width, half, sa, ra, sb, rb, sc, rc, u, out), (ca, cb) in zip(jobs, stage_two):
+        ca.wait_recv()
+        cb.wait_recv()
+        u[:, :, :half] = (
+            ref[x, y, :, :half] + ra[0, y].astype(F32) + rb[0].astype(F32)
+        ).reshape(4, quarter // 4, half)
+        u[:, :, half:] = (
+            ref[x, y, :, half:] + ra[1, x].astype(F32) + rb[1].astype(F32)
+        ).reshape(4, quarter // 4, half)
+        copies = []
+        for number, (peer, zp) in enumerate(zip(zs, zpos)):
+            sc[number] = u[zp].astype(BF)
+            copies.append(links.start(sc.at[number], rc.at[number], peer))
+        stage_three.append(copies)
+    for made in small_three:
+        made.wait_recv()
+    smallx[8 + c] = (smallx[4] + smallx[5]) + (smallx[6] + smallx[7])
+    small_pair = links.start(smallx.at[8 + c], smallx.at[8 + c], sib)
+    gather_z = []
+    for (ref, quarter, width, half, sa, ra, sb, rb, sc, rc, u, out), copies in zip(jobs, stage_three):
+        for made in copies:
+            made.wait_recv()
+        out[x, y, z] = (
+            u[z] + rc[0].astype(F32) + rc[1].astype(F32) + rc[2].astype(F32)
+        ).astype(BF)
+        gather_z.append([links.start(out.at[x, y, z], out.at[x, y, z], peer) for peer in zs])
+    gather_one = []
+    for (ref, quarter, width, half, sa, ra, sb, rb, sc, rc, u, out), copies in zip(jobs, gather_z):
+        for made in copies:
+            made.wait_recv()
+        lo, hi = pl.ds(0, half), pl.ds(half, half)
+        gather_one.append((
+            links.start(out.at[x, y, :, :, lo], out.at[x, y, :, :, lo], to_y),
+            links.start(out.at[x, y, :, :, hi], out.at[x, y, :, :, hi], to_x),
+        ))
+    gather_two = []
+    for (ref, quarter, width, half, sa, ra, sb, rb, sc, rc, u, out), (ca, cb) in zip(jobs, gather_one):
+        ca.wait_recv()
+        cb.wait_recv()
+        lo, hi = pl.ds(0, half), pl.ds(half, half)
+        gather_two.append((
+            links.start(out.at[x, :, :, :, lo], out.at[x, :, :, :, lo], to_x),
+            links.start(out.at[:, y, :, :, hi], out.at[:, y, :, :, hi], to_y),
+        ))
+    stores = []
+    pair_stores = []
+
+    def store(src, dst):
+        made = pltpu.make_async_copy(src, dst, local_sem.at[len(loads) + len(stores)])
+        made.start()
+        stores.append(made)
+        pair_stores.append(links.start(src, dst, sib))
+
+    for at, ((ref, quarter, width, half, sa, ra, sb, rb, sc, rc, u, out), (ca, cb)) in enumerate(zip(jobs, gather_two)):
+        ca.wait_recv()
+        cb.wait_recv()
+        if at == 0:
+            store(out, gup_out.at[:, :, :, :, pl.ds(wide_own, HALF)])
+        elif at == 1:
+            store(out, gdown_out.at[c])
+        elif at == 2:
+            for third in range(3):
+                store(
+                    out.at[:, :, :, :, pl.ds(third * FEAT, FEAT)],
+                    gqkv_out.at[:, :, :, :, pl.ds(pl.multiple_of(third * WIDE + own, FEAT), FEAT)],
+                )
+        else:
+            store(out, gout_out.at[c])
+    small_pair.wait_recv()
+    small_out[...] = smallx[8:10]
+    for made in stores:
+        made.wait()
+    for made in pair_stores:
+        made.wait_recv()
+    links.drain()
+
+    @pl.when(moved)
+    def _():
+        for made in swaps:
+            made.wait_send()
+        for made in (fin_copy, ig_copy):
+            made.wait_recv()
+            made.wait_send()
+
+
+GRAD_SHAPES = ((WIDE, HALF), (HALF, WIDE), (WIDE, 3 * FEAT), (FEAT, WIDE))
+
+
+def fused_scratch():
+    v = pltpu.VMEM
+    P2 = PONDER
+    groups = lambda make: [make(r, k) for r, k in GRAD_SHAPES]
+    return [
+        pltpu.SemaphoreType.DMA((N_LINKS,)),
+        pltpu.SemaphoreType.DMA((N_LINKS,)),
+        pltpu.SemaphoreType.DMA((16,)),
+        v((WIDE, 3 * FEAT), BF), v((FEAT, WIDE), BF), v((WIDE, HALF), BF), v((HALF, WIDE), BF),
+        v((2, TOK, WIDE), BF), v((2, TOK, WIDE), BF), v((2, TOK, 128), F32),
+        v((P2 + 1, ROWS, WIDE), F32), v((P2, ROWS, WIDE), BF), v((P2, QROWS, FEAT), BF),
+        v((P2, SLOTS, KEYS, WIDE), BF), v((P2, FEAT, ROWS), F32), v((P2, FEAT, ROWS), BF),
+        v((P2, ROWS, WIDE), F32), v((P2, ROWS, 1), F32), v((P2 + 1, ROWS, WIDE), BF),
+        v((P2, ROWS, HALF), BF), v((P2, ROWS, HALF), F32), v((P2, ROWS, WIDE), F32),
+        v((P2, ROWS, 1), F32), v((P2, 1, QROWS), F32),
+        v((KEYS, QROWS), F32), v((KEYS, QROWS), F32), v((KEYS, QROWS), BF), v((KEYS, QROWS), BF),
+        v((SLOTS, QROWS), F32), v((SLOTS, QROWS), F32), v((SLOTS, FEAT, ROWS), F32),
+        v((1, QROWS), F32), v((QROWS, FEAT), BF),
+        v((4 * P2, ROWS, WIDE), F32), v((4 * P2, ROWS, WIDE), F32), v((ROWS, WIDE), F32),
+        v((ROWS, WIDE), F32), v((FEAT, ROWS), F32), v((KEYS, WIDE), F32),
+        v((P2, 3, KEYS, WIDE), BF), v((P2, 3, KEYS, WIDE), BF), v((ROWS, 3 * FEAT), BF),
+        v((16, WIDE), F32),
+        v((2, 2, HALF // 4, WIDE), F32), v((2, 2, WIDE // 4, HALF), F32),
+        v((2, 2, WIDE // 4, 3 * FEAT), F32), v((2, 2, FEAT // 4, WIDE), F32),
+        groups(lambda r, k: v((2, 2, r // 4, k // 2), BF)),
+        groups(lambda r, k: v((2, 2, r // 4, k // 2), BF)),
+        groups(lambda r, k: v((2, r // 4, k // 2), BF)),
+        groups(lambda r, k: v((2, r // 4, k // 2), BF)),
+        groups(lambda r, k: v((3, r // 16, k), BF)),
+        groups(lambda r, k: v((3, r // 16, k), BF)),
+        groups(lambda r, k: v((4, r // 16, k), F32)),
+        groups(lambda r, k: v((2, 2, 4, r // 16, k), BF)),
+        v((10, 16, WIDE), F32), v((ROWS, WIDE), F32), v((ROWS, WIDE), F32),
+    ]
+
+
+def fused_local(
+    states, w_qkv, qv_bias, output_weight, out_bias, w_up, up_bias, w_down, down_bias,
+    norm_gain, norm_shift, halt_weight, halt_bias, cotangent, lengths, caps,
+):
+    vec = jnp.concatenate(
+        [
+            qv_bias, out_bias[None], up_bias.reshape(4, WIDE), down_bias[None], norm_gain, norm_shift,
+            halt_weight[None], jnp.broadcast_to(halt_bias[None], (1, WIDE)),
+            jnp.zeros((2, WIDE), F32),
+        ],
+        axis=0,
+    )
+    lane = lax.broadcasted_iota(jnp.int32, (TOK, 128), 1)
+    aux = jnp.where(
+        lane == 0, caps.reshape(TOK, 1), jnp.where(lane == 1, lengths.reshape(1, 1), 0)
+    ).astype(F32)
+    vm = pl.BlockSpec(memory_space=pltpu.VMEM)
+    hbm = pl.BlockSpec(memory_space=pl.ANY)
+    outs = pl.pallas_call(
+        fused_kernel,
+        out_shape=(
+            jax.ShapeDtypeStruct((TOK, WIDE), F32),
+            jax.ShapeDtypeStruct((TOK, WIDE), F32),
+            jax.ShapeDtypeStruct((2, 16, WIDE), F32),
+            jax.ShapeDtypeStruct((2, 2, 4, WIDE // 16, 3 * WIDE), BF),
+            jax.ShapeDtypeStruct((2, 2, 2, 4, FEAT // 16, WIDE), BF),
+            jax.ShapeDtypeStruct((2, 2, 4, WIDE // 16, 2 * HALF), BF),
+            jax.ShapeDtypeStruct((2, 2, 2, 4, HALF // 16, WIDE), BF),
+        ),
+        in_specs=[vm] * 4 + [hbm] * 4,
+        out_specs=[vm] * 3 + [hbm] * 4,
+        scratch_shapes=fused_scratch(),
+        compiler_params=pltpu.CompilerParams(
+            collective_id=0, has_side_effects=True, vmem_limit_bytes=62 * 2**20
+        ),
+        name="ponder",
+    )(states[0], cotangent[0], aux, vec, w_qkv, output_weight, w_up, w_down)
+    final, igrad, small, gqkv, gout, gup, gdown = outs
+    pick = small[0]
+    both = lambda i: jnp.concatenate([small[0, i], small[1, i]], axis=-1)
+    grad_qv = jnp.stack(
+        [
+            jnp.concatenate([small[0, 0, :FEAT], small[1, 0, :FEAT]]),
+            jnp.concatenate([small[0, 0, FEAT:], small[1, 0, FEAT:]]),
+        ]
+    )
+    return (
+        final[None],
+        igrad[None],
+        gqkv.reshape(WIDE, 3 * WIDE).astype(F32),
+        grad_qv,
+        gout.reshape(WIDE, WIDE).astype(F32),
+        pick[1],
+        gup.reshape(WIDE, 2 * HALF).astype(F32),
+        small[:, 2:4].reshape(2 * HALF),
+        gdown.reshape(2 * HALF, WIDE).astype(F32),
+        pick[4],
+        pick[5:7],
+        pick[7:9],
+        pick[9],
+        pick[10, :1],
+    )
+
+
+SPECS_IN = (
+    P("dp", "seq", None),) + (P(),) * 12 + (P("dp", "seq", None), P("dp"), P("dp", "seq"))
+SPECS_OUT = (P("dp", "seq", None),) * 2 + (P(),) * 12
+
+
 def solution(mesh):
-    return jax.shard_map(
-        local,
-        mesh=mesh,
-        in_specs=(
-            P("dp", "seq", None),
-            P(),
-            P(),
-            P(),
-            P(),
-            P(),
-            P(),
-            P(),
-            P(),
-            P(),
-            P(),
-            P(),
-            P(),
-            P("dp", "seq", None),
-            P("dp"),
-            P("dp", "seq"),
-        ),
-        out_specs=(
-            P("dp", "seq", None),
-            P("dp", "seq", None),
-            P(),
-            P(),
-            P(),
-            P(),
-            P(),
-            P(),
-            P(),
-            P(),
-            P(),
-            P(),
-            P(),
-            P(),
-        ),
-        check_vma=False,
-    )
+    square = mesh.shape["dp"] == 4 and mesh.shape["seq"] == 8
+
+    def whole(*arrays):
+        states, w_up = arrays[0], arrays[5]
+        fits = square and states.shape == (4, 8 * TOK, WIDE) and w_up.shape == (WIDE, 2 * HALF)
+        return jax.shard_map(
+            fused_local if fits else local,
+            mesh=mesh,
+            in_specs=SPECS_IN,
+            out_specs=SPECS_OUT,
+            check_vma=False,
+        )(*arrays)
+
+    return whole

time: 609 us -> 222 us (0.36)
  waiting for transfers between devices: 400 us -> 0 us
  Pallas kernels: 0 us -> 196 us
  local copies, waits for them, and re-layouts: 63.5 us -> 11 us
  matrix products: 51.9 us -> 0 us
  blocking collectives: 43.6 us -> 0 us
  other arithmetic: 29.8 us -> 12.3 us
  between operations: 16.1 us -> 2 us
    pallas_call x0 -> x1, Pallas kernels: none -> 196 us  [fused_local(): pl.pallas_call(fused_kernel, out_shape=(jax.ShapeDtypeStruct((TOK, WIDE),...]
    psum x1 -> x0, waiting for transfers between devices: 190 us -> none  [local(): lax.psum((totals[0], totals[1], totals[2], totals[3], totals[4], totals[5...]
    reduce_scatter x4 -> x0, waiting for transfers between devices: 124 us -> none  [the longest x2 70.8 us: attend_back(): lax.psum_scatter(grad_key_all, 'seq', scatter_dimension=1, tiled=True)]
    all_gather x4 -> x0, waiting for transfers between devices: 84.9 us -> none  [the longest x2 44 us: attend(): key_piece = lax.all_gather(key_rows, 'seq', axis=1, tiled=True)]
    dot_general x52 -> x0, matrix products: 51.9 us -> none  [the longest x8 5.57 us: one_block(): jnp.einsum('sqhe,skhe->shqk', query_heads, key_block, preferred_element_t...]
    psum x1 -> x0, blocking collectives: 43.6 us -> none  [local(): lax.psum((totals[0], totals[1], totals[2], totals[3], totals[4], totals[5...]
    unnamed x274 -> x14, local copies, waits for them, and re-layouts: 25 us -> 2.79 us
    reduce_sum x26 -> x0, other arithmetic: 15.9 us -> none  [the longest x2 3.82 us: backward_block(): jnp.sum(grad_mixed[..., 2 * model_width:].astype(jnp.float32), axis=(0, 1))]
  transfers between devices with their start and end apart: 9 -> 0, of which waited for: 9 -> 0; matrix products, arithmetic and copies ran while one was open for 4% -> 0% of each run, Pallas kernels for 0% -> 0%
where the time goes in v1:
time: 222 us; the launch traced here: 221 us
  Pallas kernels  196 us (88%)
  other arithmetic  12.3 us (6%)
  local copies, waits for them, and re-layouts  11 us (5%)
    pallas_call x1, Pallas kernels, fused_local(): pl.pallas_call(fused_kernel, out_shape=(jax.ShapeDtypeStruct((TOK, WIDE),...  196 us

profile of v1, /device:TPU:1, one launch (start us, length us, event | category | flops | bytes accessed | tf_op | source)
XLA Modules:
  0.0 221.1 jit_solution(15958274861319617952)
XLA Ops:
  1.3 1.4 select_convert_fusion.aux_in
  2.7 0.7 reshape.61
  4.1 2.7 %concatenate.9.vec = f32[16,512]{1,0:T(8,128)} concatenate(f32[2,512]{1,0:T(2,128)} %param.18, f32[1,512]{1,0:T(1,128)} %bitcast.54, f32[4,512]{1,0:T(4,128)S(1)} %reshape.61, f32[1,512]{1,0:T(1,128)} %bitcast.55, f32[2,512]{1,0:T(2,128)} %param.25, f32[2,512]{1,0:T(2,128)} %param.26, f32[1,512]{1,0:T(1,128)} %bitcast.56, f32[1,512]{1,0:T(1,128)S(1)} %broadcast_in_dim.56, ...), dimensions={0} | concatenate | bytes 65536 | tf_op jit(solution)/shard_map/concatenate | solution.py:1010
  6.7 195.8 %ponder.1 = (f32[128,512]{1,0:T(8,128)}, f32[128,512]{1,0:T(8,128)}, f32[2,16,512]{2,1,0:T(8,128)}, bf16[2,2,4,32,1536]{4,3,2,1,0:T(8,128)(2,1)}, bf16[2,2,2,4,1...) custom-call(bf16[128,512]{1,0:T(8,128)(2,1)} %bitcast.45, ...), custom_call_target="tpu_custom_call" | custom-call | tf_op jit(solution)/shard_map/ponder/pallas_call | solution.py:1024
  202.6 0.8 fusion.1
  203.4 0.6 pad_maximum_fusion
  204.0 1.4 fusion
  205.3 1.4 slice_bitcast_fusion.2
  206.7 0.8 slice_bitcast_fusion
  207.5 0.5 slice.64
  208.0 0.8 slice_bitcast_fusion.1
  208.8 0.6 copy.30
  209.4 0.0 copy-start
  209.4 4.3 %bitcast_convert_fusion = f32[2048,512]{1,0:T(8,128)} fusion(bf16[2,2,2,4,64,512]{5,4,3,2,1,0:T(8,128)(2,1)} %get-tuple-element.27), kind=kLoop, calls=%fused_computation | loop fusion | flops 1048576 | bytes 6291456 | tf_op jit(solution)/shard_map/convert_element_type | solution.py:1061
  213.7 0.0 copy-done
  213.7 0.0 copy-start.1
  213.7 2.7 %bitcast_convert_fusion.1 = f32[512,2048]{1,0:T(8,128)} fusion(bf16[2,2,4,32,2048]{4,3,2,1,0:T(8,128)(2,1)S(1)} %copy-done), kind=kLoop, calls=%fused_computation.1 | loop fusion | flops 1048576 | bytes 6291456 | tf_op jit(solution)/shard_map/convert_element_type | solution.py:1059
  216.4 0.0 copy-done.1
  216.4 0.0 copy-start.2
  216.4 0.0 copy-start.4
  216.4 2.2 bitcast_convert_fusion.2
  218.6 0.0 copy-start.3
  218.6 0.0 copy-done.2
  218.6 1.1 bitcast_convert_fusion.3
  219.7 0.0 copy-done.4
  219.7 0.7 copy.35
  220.4 0.0 copy-done.3
  220.4 0.7 copy.36
  (6 shorter events, 0.0 us)
Async XLA Ops:
  209.4 4.4 %copy-start = (bf16[2,2,4,32,2048]{4,3,2,1,0:T(8,128)(2,1)S(1)}, bf16[2,2,4,32,2048]{4,3,2,1,0:T(8,128)(2,1)}, u32[]{:S(2)}) copy-start(bf16[2,2,4,32,2048]{4,3,2,1,0:T(8,128)(2,1)} %get-tuple-element.26) | copy-start | bytes 6291460
  213.7 2.7 %copy-start.1 = (bf16[2,2,4,32,1536]{4,3,2,1,0:T(8,128)(2,1)S(1)}, bf16[2,2,4,32,1536]{4,3,2,1,0:T(8,128)(2,1)}, u32[]{:S(2)}) copy-start(bf16[2,2,4,32,1536]{4,3,2,1,0:T(8,128)(2,1)} %get-tuple-element.23) | copy-start | bytes 4718596
  216.4 2.2 copy-start.2
  216.4 3.3 %copy-start.4 = (f32[128,512]{1,0:T(8,128)S(1)}, f32[128,512]{1,0:T(8,128)}, u32[]{:S(2)}) copy-start(f32[128,512]{1,0:T(8,128)} %get-tuple-element.21) | copy-start | bytes 786436
  218.6 1.9 copy-start.3

commit v2 on v0

--- a/solution.py
+++ b/solution.py
@@ -1,8 +1,11 @@
+import functools
 import math
 
 import jax
 import jax.numpy as jnp
 from jax import lax
+from jax.experimental import pallas as pl
+from jax.experimental.pallas import tpu as pltpu
 from jax.sharding import PartitionSpec as P
 
 HEADS = 8
@@ -413,43 +416,922 @@
     return (final_state, grad_state) + tuple(summed)
 
 
+BF = jnp.bfloat16
+F32 = jnp.float32
+MESH = pl.DeviceIdType.MESH
+GELU_A = math.sqrt(2.0 / math.pi)
+GELU_B = 0.044715
+TOK = 128
+ROWS = 256
+WIDE = 512
+HALF = 1024
+FEAT = 256
+HEADC = 4
+BLOCKS = 4
+PAIR = 2
+SEQ = BLOCKS * ROWS
+QROWS = HEADC * ROWS
+CHUNK = 128
+BAND = 64
+SAVED = BLOCKS + PAIR
+HEAD = FEAT // HEADC
+
+UNITS = ((64, 128),) * 8 + ((32, 256),) * 3 + ((16, 512),)
+PLAN = (
+    ("xy2", "y12x"),
+    ("2D", "12D"),
+    ("D2", "ZD"),
+    ("2D", "DZ"),
+    ("xy2", "x21y"),
+    ("y2x", "21D"),
+    ("D2", "21xy"),
+    ("y2x", "21yx"),
+    ("yx2", "DZ"),
+    ("xy2", "ZD"),
+    ("D2", "2D1"),
+    ("yx2", "ZD"),
+)
+FIRST, SECOND = range(8), range(8, 12)
+EVENTS = (
+    (),
+    (),
+    (),
+    (),
+    (0, 5,),
+    (1, 2,),
+    (4, 7,),
+    (),
+    (3, 6, 0,),
+    (5, 1,),
+    (2, 4,),
+    (7,),
+    (3, 0, 5, 1,),
+    (6,),
+    (7,),
+    (2, 0, 4,),
+    (5, 3,),
+    (),
+    (1, 6,),
+    (7, 0,),
+    (5, 4,),
+    (2,),
+    (),
+    (),
+    (1, 6, 7, 3, 5, 8, 9, 0, 4, 10, 11, 6, 8, 7, 9, 4, 0, 11, 10, 6, 8, 9, 7, 11, 4, 10, 8, 9, 11, 10, 9, 8, 10, 11,),
+)
+
+
+def axes_of(stage):
+    return {"D": "xy", "Z": "12"}.get(stage, stage)
+
+
+def nn(a, b):
+    return lax.dot_general(a, b, (((1,), (0,)), ((), ())), preferred_element_type=F32)
+
+
+def nt(a, b):
+    return lax.dot_general(a, b, (((1,), (1,)), ((), ())), preferred_element_type=F32)
+
+
+def tn(a, b):
+    return lax.dot_general(a, b, (((0,), (0,)), ((), ())), preferred_element_type=F32)
+
+
+def colsum(v):
+    return jnp.sum(v, axis=0, keepdims=True)
+
+
+def rowsum(v):
+    return jnp.sum(v, axis=1, keepdims=True)
+
+
+class Links:
+    def __init__(self, send, recv):
+        self.send, self.recv, self.used, self.open = send, recv, 0, []
+
+    def take(self, count):
+        at = self.used
+        self.used += count
+        return at
+
+    def copy(self, src, dst, device, at):
+        return pltpu.make_async_remote_copy(
+            src_ref=src,
+            dst_ref=dst,
+            send_sem=self.send.at[at],
+            recv_sem=self.recv.at[at],
+            device_id=device,
+            device_id_type=MESH,
+        )
+
+    def start(self, src, dst, device):
+        made = self.copy(src, dst, device, self.take(1))
+        made.start()
+        self.open.append(made)
+        return made
+
+    def drain(self):
+        for made in self.open:
+            made.wait_send()
+        self.open = []
+
+
+N_LINKS = 256
+
+
+def each(low, high, body):
+    def step(i, carry):
+        body(i)
+        return carry
+
+    lax.fori_loop(low, high, step, 0)
+
+
+def fused_kernel(
+    states, cot_in, caps_in, length_in, qv_bias, out_bias, up_bias, down_bias, gains, shifts, halt_w, halt_b,
+    wqkv_all, wout_all, wup_all, wdown_all,
+    final_out, igrad_out, small_out, gqkv_out, gout_out, gup_out, gdown_out,
+    send_sem, recv_sem, local_sem,
+    wqkv, wout, wup, wdown,
+    stg, ct, ax, bias, rnd, s, kk, vv, kt, vt, qq, q4, do4,
+    big, pb, logt, ctxt, ctxlt, x1, x2, rs1, rs2, n1low, hid, dgelu,
+    xs, xr, g, gmlp, gpre, dk, dv, dqt, drow, dqkv,
+    mix, glog, acc, small, smallx, ig_s, ig_r,
+    grads, sends, recvs, outs,
+):
+    dp = lax.axis_index("dp")
+    sq = lax.axis_index("seq")
+    x, y = lax.rem(dp, 2), dp // 2
+    z, c = sq // 2, lax.rem(sq, 2)
+    lo, hi = lax.rem(z, 2), z // 2
+
+    def flip(value, bit):
+        return value + bit - 2 * bit * lax.rem(value // bit, 2)
+
+    sib = (dp, flip(sq, 1))
+    to = {
+        "x": (flip(dp, 1), sq),
+        "y": (flip(dp, 2), sq),
+        "1": (dp, flip(sq, 2)),
+        "2": (dp, flip(sq, 4)),
+    }
+    far = (dp, flip(flip(sq, 2), 4))
+    across = (flip(flip(dp, 1), 2), sq)
+    peers = (sib, to["x"], to["y"], across, to["1"], to["2"], far)
+
+    loads = []
+
+    def load(src, dst):
+        made = pltpu.make_async_copy(src, dst, local_sem.at[len(loads)])
+        made.start()
+        loads.append(made)
+
+    own = pl.multiple_of(c * FEAT, FEAT)
+    wide_own = pl.multiple_of(c * HALF, HALF)
+    for third in range(3):
+        load(
+            wqkv_all.at[:, pl.ds(pl.multiple_of(third * WIDE + own, FEAT), FEAT)],
+            wqkv.at[:, pl.ds(third * FEAT, FEAT)],
+        )
+    load(wout_all.at[pl.ds(own, FEAT), :], wout)
+    load(wup_all.at[:, pl.ds(wide_own, HALF)], wup)
+    load(wdown_all.at[pl.ds(wide_own, HALF), :], wdown)
+
+    barrier = pltpu.get_barrier_semaphore()
+    for peer in peers:
+        pl.semaphore_signal(barrier, inc=1, device_id=peer, device_id_type=MESH)
+    pl.semaphore_wait(barrier, len(peers))
+    links = Links(send_sem, recv_sem)
+
+    here = stg.at[z, c]
+    others = (to["1"], to["2"], far)
+    places = (flip(z, 1), flip(z, 2), flip(flip(z, 1), 2))
+    came = [links.start(states, here, peer) for peer in others]
+    beside = [links.start(states, here, sib)]
+    stg[z, c] = states[...]
+
+    row = lambda ref, i: ref[i : i + 1, :]
+    flat = lambda ref: ref[...].reshape(1, -1)
+    mine = lambda v: jnp.where(c == 0, v[:, :FEAT], v[:, FEAT:])
+    b_q, b_v = mine(row(qv_bias, 0)), mine(row(qv_bias, 1))
+    up_all = flat(up_bias)
+    b_up = jnp.where(c == 0, up_all[:, :HALF], up_all[:, HALF:])
+    b_out, b_down, w_halt = flat(out_bias), flat(down_bias), flat(halt_w)
+    lane_head = lax.broadcasted_iota(jnp.int32, (1, FEAT), 1) // HEAD
+    key_at = lax.broadcasted_iota(jnp.int32, (SEQ, ROWS), 0)
+    bias[...] = jnp.where(key_at < length_in[0], 0.0, MASK_FILL)
+    caps_row = caps_in[...].astype(F32)
+    ax[lo, c] = jnp.broadcast_to(caps_row, (TOK, 128)).T
+    acc[...] = jnp.zeros_like(acc)
+    small[...] = jnp.zeros_like(small)
+    for made in loads:
+        made.wait()
+
+    def block(ref, b):
+        return ref[b].reshape(ROWS, WIDE)
+
+    def queries(n, at, rounded):
+        q = (nn(rounded, wqkv[:, :FEAT]) + b_q).astype(BF)
+        qq[at] = (q.astype(F32) * 0.125).astype(BF)
+
+    def keys(n, b, rounded):
+        kk[n, b] = nn(rounded, wqkv[:, FEAT : 2 * FEAT]).astype(BF)
+        value = (nn(rounded, wqkv[:, 2 * FEAT :]) + b_v).astype(BF)
+        vv[n, b] = value
+        vt[:, pl.ds(pl.multiple_of(b * ROWS, ROWS), ROWS)] = value.T
+
+    beside[0].wait_recv()
+    queries(0, z, block(stg, z))
+    keys(0, z, block(stg, z))
+    for made, place in zip(came, places):
+        made.wait_recv()
+        beside.append(links.start(stg.at[place, c], stg.at[place, c], sib))
+    for made, place in zip(beside[1:], places):
+        made.wait_recv()
+        queries(0, place, block(stg, place))
+        keys(0, place, block(stg, place))
+
+    links_pair = []
+    for src, ref in ((cot_in, ct), (ax.at[lo, c], ax)):
+        links_pair.append((ref, links.start(src, ref.at[lo, c], to["1"]), links.start(src, ref.at[lo, c], sib)))
+    ct[lo, c] = cot_in[...]
+
+    def stack_heads(ref, value):
+        for h in range(HEADC):
+            ref[h * ROWS : (h + 1) * ROWS, :] = jnp.where(lane_head == h, value, jnp.zeros_like(value))
+
+    def attention(n, at):
+        stack_heads(q4, qq[at])
+        key_all = kk[n].reshape(SEQ, FEAT)
+        heads = [slice(h * ROWS, (h + 1) * ROWS) for h in range(HEADC)]
+
+        def head_scores(h):
+            big[:, heads[h % 2]] = nt(key_all, q4[heads[h], :])
+
+        head_scores(0)
+        for h, cut in enumerate(heads):
+            buf = heads[h % 2]
+            if h + 1 < HEADC:
+                head_scores(h + 1)
+            top = None
+            for b in range(BLOCKS):
+                r = slice(b * ROWS, (b + 1) * ROWS)
+                m = jnp.max(big[r, buf] + bias[r, :], axis=0, keepdims=True)
+                top = m if top is None else jnp.maximum(top, m)
+            total = None
+            for b in range(BLOCKS):
+                r = slice(b * ROWS, (b + 1) * ROWS)
+                e = jnp.exp(big[r, buf] + bias[r, :] - top)
+                pb[r, buf] = e.astype(BF)
+                total = colsum(e) if total is None else total + colsum(e)
+            logt[at, :, cut] = top + jnp.log(total)
+            hr = slice(h * HEAD, (h + 1) * HEAD)
+            ctxt[at, hr, :] = nn(vt[hr, :], pb[:, buf]) * (1.0 / total)
+        low = ctxt[at].astype(BF)
+        ctxlt[:, pl.ds(pl.multiple_of(at * ROWS, ROWS), ROWS)] = low
+        return tn(low, wout[...])
+
+    SLOT_A, SLOT_M = 0, BLOCKS
+
+    def swap_out(slot, i, first_sem, value):
+        xs[slot + i] = value.astype(BF)
+        links.copy(xs.at[slot + i], xr.at[slot + i], sib, first_sem + i).start()
+
+    def swap_in(slot, i, first_sem):
+        links.copy(xs.at[slot + i], xr.at[slot + i], sib, first_sem + i).wait()
+
+    def swapped(slot, i, band):
+        return xs[slot + i, band, :].astype(F32) + xr[slot + i, band, :].astype(F32)
+
+    def norm(resid):
+        centered = resid - jnp.mean(resid, axis=1, keepdims=True)
+        scale = lax.rsqrt(jnp.mean(centered * centered, axis=1, keepdims=True) + NORM_EPSILON)
+        return centered * scale, scale
+
+    bands = [pl.ds(at, BAND) for at in range(0, ROWS, BAND)]
+    cores = [(at // TOK, pl.ds(at % TOK, BAND)) for at in range(0, ROWS, BAND)]
+    base = PAIR * hi
+
+    def place_of(n, i):
+        return i if n == 0 else base + i
+
+    def saved_of(n, i):
+        return i if n == 0 else BLOCKS + i
+
+    def caps_of(i, part):
+        return ax[i, part[0], part[1], 0:1]
+
+    def forward(n):
+        count = BLOCKS if n == 0 else PAIR
+        sem_a, sem_m = links.take(count), links.take(count)
+        each(0, count, lambda i: swap_out(SLOT_A, i, sem_a, attention(n, saved_of(n, i))))
+
+        def middle(i):
+            swap_in(SLOT_A, i, sem_a)
+            at, place = saved_of(n, i), place_of(n, i)
+            for band, part in zip(bands, cores):
+                state = stg[place, part[0], part[1], :].astype(F32) if n == 0 else s[place, band, :]
+                hat, scale = norm(state + swapped(SLOT_A, i, band) + b_out)
+                x1[at, band, :] = hat
+                rs1[at, band, :] = scale
+                normed = hat * row(gains, 0) + row(shifts, 0)
+                g[place, band, :] = normed
+                n1low[at, band, :] = normed.astype(BF)
+            for half in range(2):
+                cols = slice(half * WIDE, (half + 1) * WIDE)
+                big[half * ROWS : (half + 1) * ROWS, :] = nn(n1low[at], wup[:, cols]) + b_up[:, cols]
+            for half in range(2):
+                cols = slice(half * WIDE, (half + 1) * WIDE)
+                for start in range(0, ROWS, BAND):
+                    band = slice(start, start + BAND)
+                    v = big[half * ROWS + start : half * ROWS + start + BAND, :]
+                    v2 = v * v
+                    t = jnp.tanh(GELU_A * v * (1.0 + GELU_B * v2))
+                    up = 0.5 * (1.0 + t)
+                    hid[at, band, cols] = (v * up).astype(BF)
+                    dgelu[at, band, cols] = (
+                        up + (0.5 * GELU_A) * v * (1.0 - t * t) * (1.0 + (3.0 * GELU_B) * v2)
+                    ).astype(dgelu.dtype)
+            swap_out(SLOT_M, i, sem_m, nn(hid[at], wdown[...]))
+
+        each(0, count, middle)
+
+        def last(i):
+            swap_in(SLOT_M, i, sem_m)
+            at, place = saved_of(n, i), place_of(n, i)
+            for band, part in zip(bands, cores):
+                hat, scale = norm(g[place, band, :] + swapped(SLOT_M, i, band) + b_down)
+                x2[at, band, :] = hat
+                rs2[at, band, :] = scale
+                updated = hat * row(gains, 1) + row(shifts, 1)
+                if n == 0:
+                    s[place, band, :] = updated
+                    rnd[place, band, :] = updated.astype(BF)
+                else:
+                    g[place, band, :] = jnp.where(caps_of(i, part) > n, updated, s[place, band, :])
+
+        each(0, count, last)
+
+    forward(0)
+    for ref, from_pair, from_sib in links_pair:
+        from_pair.wait_recv()
+        from_sib.wait_recv()
+    onward = [links.start(ref.at[1 - lo, c], ref.at[1 - lo, c], sib) for ref, _, _ in links_pair]
+    each(0, BLOCKS, lambda b: keys(1, b, rnd[b]))
+    each(0, PAIR, lambda i: queries(1, BLOCKS + i, rnd[base + i]))
+    for made in onward:
+        made.wait_recv()
+    forward(1)
+
+    mine_rows = pl.ds(pl.multiple_of(c * TOK, TOK), TOK)
+
+    def halting(i):
+        place = base + i
+        first = stg[place].reshape(ROWS, WIDE).astype(F32)
+        halt = jax.nn.sigmoid(rowsum(first * w_halt) + halt_b[0])
+        more = ax[i].reshape(ROWS, 128)[:, 0:1] > 1.0
+        mix[0, i] = jnp.where(more, halt, 1.0)
+        mix[1, i] = jnp.where(more, 1.0 - halt, 0.0)
+        cot = ct[i].reshape(ROWS, WIDE).astype(F32)
+        through = jnp.where(more, rowsum(cot * s[place]) - rowsum(cot * g[place]) - PONDER_COST, 0.0)
+        logit = through * halt * (1.0 - halt)
+        glog[i] = logit
+        acc[72:80, :] += jnp.sum((logit * first).reshape(ROWS // 8, 8, WIDE), axis=0)
+        acc[80:81, :] += jnp.broadcast_to(colsum(logit), (1, WIDE))
+
+    each(0, PAIR, halting)
+    final_out[...] = mix[0, lo, mine_rows, :] * s[z, mine_rows, :] + mix[1, lo, mine_rows, :] * g[z, mine_rows, :]
+    g[...] = jnp.zeros_like(g)
+
+    def start_grad(i):
+        g[base + i] = ct[i].reshape(ROWS, WIDE).astype(F32) * mix[1, i]
+
+    each(0, PAIR, start_grad)
+
+    def norm_back(grad, hat, scale, gain):
+        v = grad * gain
+        a = jnp.mean(v, axis=1, keepdims=True)
+        b = jnp.mean(v * hat, axis=1, keepdims=True)
+        return scale * (v - a - hat * b)
+
+    def add_small(at, value, first_col=0):
+        rows, width = value.shape
+        cols = slice(first_col, first_col + width)
+        acc[at * 8 : at * 8 + 8, cols] += jnp.sum(value.reshape(rows // 8, 8, width), axis=0)
+
+    def add_unit(unit, value, fresh):
+        ref = grads[unit]
+        value = value.reshape(ref.shape)
+        if fresh:
+            ref[...] = value
+        else:
+            ref[...] += value
+
+    half_cols = pl.ds(pl.multiple_of(lo * WIDE, WIDE), WIDE)
+
+    def backward_mlp(n, fresh):
+        count = BLOCKS if n == 0 else PAIR
+        sem_a = links.take(count)
+        first, end = (0, BLOCKS) if n == 0 else (BLOCKS, SAVED)
+
+        def one(i):
+            at, place = saved_of(n, i), place_of(n, i)
+            for band, part in zip(bands, cores):
+                grad = g[place, band, :]
+                if n > 0:
+                    grad = jnp.where(caps_of(i, part) > n, grad, 0.0)
+                hat = x2[at, band, :]
+                back = norm_back(grad, hat, rs2[at, band, :], row(gains, 1))
+                g[place, band, :] = back
+                add_small(6, grad * hat)
+                add_small(8, grad)
+                rounded = back.astype(BF)
+                add_small(4, rounded.astype(F32))
+                gmlp[i, band, :] = rounded
+            for half in range(2):
+                rows = slice(half * WIDE, (half + 1) * WIDE)
+                big[half * ROWS : (half + 1) * ROWS, :] = nt(gmlp[i], wdown[rows, :])
+            for half in range(2):
+                cols = slice(half * WIDE, (half + 1) * WIDE)
+                for start in range(0, ROWS, BAND):
+                    band = slice(start, start + BAND)
+                    above = big[half * ROWS + start : half * ROWS + start + BAND, :]
+                    grad = (dgelu[at, band, cols].astype(F32) * above).astype(BF)
+                    gpre[i, band, cols] = grad
+                    add_small(2 + half, grad.astype(F32))
+            swap_out(SLOT_A, i, sem_a, nt(gpre[i], wup[...]))
+
+        each(0, count, one)
+        length = count * ROWS
+        down = tn(hid[first:end, :, half_cols].reshape(length, WIDE), gmlp[:count].reshape(length, WIDE))
+        for k in range(4):
+            add_unit(4 + k, down[:, k * 128 : (k + 1) * 128], fresh)
+        up = tn(n1low[first:end].reshape(length, WIDE), gpre[:count, :, half_cols].reshape(length, WIDE))
+        for k in range(4):
+            add_unit(k, up[:, k * 128 : (k + 1) * 128], fresh)
+        return sem_a
+
+    def backward_norm(n, sem_a, beat=None):
+        count = BLOCKS if n == 0 else PAIR
+
+        def one(i):
+            swap_in(SLOT_A, i, sem_a)
+            at, place = saved_of(n, i), place_of(n, i)
+            for band in bands:
+                grad = g[place, band, :] + swapped(SLOT_A, i, band)
+                hat = x1[at, band, :]
+                back = norm_back(grad, hat, rs1[at, band, :], row(gains, 0))
+                g[place, band, :] = back
+                add_small(5, grad * hat)
+                add_small(7, grad)
+                rounded = back.astype(BF)
+                add_small(1, rounded.astype(F32))
+                gmlp[i, band, :] = rounded
+
+        if beat is None:
+            each(0, count, one)
+        else:
+            for i in range(count):
+                one(i)
+                beat()
+        kt[...] = kk[n].reshape(SEQ, FEAT).T
+        dk[...] = jnp.zeros_like(dk)
+        dv[...] = jnp.zeros_like(dv)
+        if n > 0:
+            dqkv[:, :, :FEAT] = jnp.zeros((BLOCKS, ROWS, FEAT), BF)
+
+    def backward_heads(n, i):
+        at, place = saved_of(n, i), place_of(n, i)
+        stack_heads(q4, qq[at])
+        stack_heads(do4, nt(gmlp[i], wout[...]).astype(BF))
+        dots = nt(wout[...], gmlp[i]).astype(BF).astype(F32) * ctxt[at]
+        for h in range(HEADC):
+            drow[:, h * ROWS : (h + 1) * ROWS] = colsum(dots[h * HEAD : (h + 1) * HEAD, :])
+
+    span = SEQ // 2
+    PARTS = 4
+
+    def backward_part(n, i, part):
+        at, place = saved_of(n, i), place_of(n, i)
+        side, pair = part // 2, part % 2
+        b0 = side * BLOCKS // 2
+        keys_here = slice(b0, b0 + BLOCKS // 2)
+        rows_here = slice(side * span, (side + 1) * span)
+        cols = slice(pair * WIDE, (pair + 1) * WIDE)
+        big[:span, :] = nt(kk[n, keys_here].reshape(span, FEAT), q4[cols, :])
+        big[span:, :] = nt(vv[n, keys_here].reshape(span, FEAT), do4[cols, :])
+        for cut_at in range(0, WIDE, CHUNK):
+            cut = slice(cut_at, cut_at + CHUNK)
+            q_cut = slice(pair * WIDE + cut_at, pair * WIDE + cut_at + CHUNK)
+            for at_row in range(0, span, ROWS):
+                r, r2 = slice(at_row, at_row + ROWS), slice(span + at_row, span + at_row + ROWS)
+                key_rows = slice(side * span + at_row, side * span + at_row + ROWS)
+                p = jnp.exp(big[r, cut] + bias[key_rows, :CHUNK] - logt[at, :, q_cut])
+                pb[r, cut] = p.astype(BF)
+                pb[r2, cut] = (p * (big[r2, cut] - drow[:, q_cut])).astype(BF)
+        dv[rows_here, :] += nn(pb[:span, :], do4[cols, :])
+        dk[rows_here, :] += nn(pb[span:, :], q4[cols, :])
+        for h in range(2):
+            head = 2 * pair + h
+            hr = slice(head * HEAD, (head + 1) * HEAD)
+            term = nn(kt[hr, rows_here], pb[span:, h * ROWS : (h + 1) * ROWS])
+            if side == 0:
+                dqt[hr, :] = term
+            else:
+                dqt[hr, :] += term
+        if part == PARTS - 1:
+            dqkv[place, :, :FEAT] = (dqt[...] * 0.125).T.astype(BF)
+
+    def backward_attention(n, i):
+        backward_heads(n, i)
+        for part in range(PARTS):
+            backward_part(n, i, part)
+
+    def backward_rest(n, fresh, beat=None):
+        count = BLOCKS if n == 0 else PAIR
+        sem_m = links.take(BLOCKS)
+        dqkv[:, :, FEAT : 2 * FEAT] = dk[...].reshape(BLOCKS, ROWS, FEAT).astype(BF)
+        dqkv[:, :, 2 * FEAT :] = dv[...].reshape(BLOCKS, ROWS, FEAT).astype(BF)
+        if beat is None:
+            each(0, BLOCKS, lambda b: swap_out(SLOT_M, b, sem_m, nt(dqkv[b], wqkv[...])))
+        else:
+            for b in range(BLOCKS):
+                swap_out(SLOT_M, b, sem_m, nt(dqkv[b], wqkv[...]))
+                beat()
+        length = count * ROWS
+        at = 0 if n == 0 else SEQ
+        side = ctxlt[pl.ds(pl.multiple_of(lo * TOK, TOK), TOK), at : at + length]
+        add_unit(11, nn(side, gmlp[:count].reshape(length, WIDE)), fresh)
+        grad = dqkv[...].reshape(SEQ, 3 * FEAT)
+        add_small(0, grad[:, :FEAT].astype(F32))
+        add_small(0, grad[:, 2 * FEAT :].astype(F32), FEAT)
+        quarter = pl.ds(pl.multiple_of(lo * ROWS, ROWS), ROWS)
+        source = stg[:, :, :, quarter] if n == 0 else rnd[:, :, quarter]
+        total = tn(source.reshape(SEQ, ROWS), grad)
+        for k in range(3):
+            add_unit(8 + k, total[:, k * FEAT : (k + 1) * FEAT], fresh)
+        return sem_m
+
+    def backward_end(sem_m):
+        def one(b):
+            swap_in(SLOT_M, b, sem_m)
+            for band in bands:
+                g[b, band, :] += swapped(SLOT_M, b, band)
+
+        each(0, BLOCKS, one)
+
+    sem = backward_mlp(1, True)
+    backward_norm(1, sem)
+    each(0, PAIR, lambda i: backward_attention(1, i))
+    backward_end(backward_rest(1, True))
+
+    def add_first(i):
+        cot = ct[i].reshape(ROWS, WIDE).astype(F32)
+        active = ax[i].reshape(ROWS, 128)[:, 0:1] > 1.0
+        passed = jnp.where(active, 0.0, cot * mix[1, i])
+        g[base + i] = g[base + i] + passed + cot * mix[0, i]
+
+    each(0, PAIR, add_first)
+
+    place_on = {"x": x, "y": y, "1": lo, "2": hi}
+    RS_DIMS, AG_DIMS = "2xy", "12xy"
+    flip_of = {"x": (1, 0), "y": (2, 0), "1": (0, 2), "2": (0, 4)}
+
+    def pick(dims, fixed):
+        return tuple(fixed.get(d, slice(None)) for d in dims)
+
+    def toward(dims):
+        at_dp, at_sq = dp, sq
+        for d in dims:
+            one, two = flip_of[d]
+            at_dp = flip(at_dp, one) if one else at_dp
+            at_sq = flip(at_sq, two) if two else at_sq
+        return (at_dp, at_sq)
+
+    def subsets(dims):
+        return [dims] if len(dims) == 1 else [dims[:1], dims[1:], dims]
+
+    class Unit:
+        def __init__(self, number):
+            self.number = number
+            reduce, gather = PLAN[number]
+            self.count = len(reduce) + len(gather)
+            self.stages = []
+            fixed = {}
+            left = {d: place_on[d] for d in AG_DIMS}
+            for at, dims in enumerate(map(axes_of, reduce + gather)):
+                reducing = at < len(reduce)
+                copies, cuts = [], []
+                for which, some in enumerate(subsets(dims)):
+                    if reducing:
+                        cut = dict(fixed)
+                        for d in dims:
+                            cut[d] = 1 - place_on[d] if d in some else place_on[d]
+                        cuts.append(cut)
+                        src, dst = sends[number][at][which], recvs[number][at][which]
+                    else:
+                        src = dst = outs[number].at[pick(AG_DIMS, left)]
+                    copies.append((src, dst, toward(some), links.take(1)))
+                for d in dims:
+                    if reducing:
+                        fixed[d] = place_on[d]
+                    else:
+                        del left[d]
+                self.stages.append((reducing, copies, cuts, dict(fixed)))
+
+        def launch(self, at):
+            reducing, copies, cuts, _ = self.stages[at]
+            for which, copy in enumerate(copies):
+                if reducing:
+                    copy[0][...] = grads[self.number][pick(RS_DIMS, cuts[which])].astype(BF)
+                links.copy(*copy).start()
+
+        def advance(self, at):
+            n = self.number
+            reducing, copies, _, fixed = self.stages[at]
+            for copy in copies:
+                links.copy(*copy).wait_recv()
+            if reducing:
+                keep = pick(RS_DIMS, fixed)
+                total = grads[n][keep]
+                for copy in copies:
+                    total = total + copy[1][...].astype(F32)
+                if len(fixed) < 3:
+                    grads[n][keep] = total
+                else:
+                    outs[n][pick(AG_DIMS, place_on)] = total.astype(BF)
+            if at + 1 < self.count:
+                self.launch(at + 1)
+            else:
+                store_unit(n)
+
+        def drain(self):
+            for _, copies, _, _ in self.stages:
+                for copy in copies:
+                    links.copy(*copy).wait_send()
+
+    stores = []
+    pair_stores = []
+
+    def store(src, dst):
+        made = pltpu.make_async_copy(src, dst, local_sem.at[len(loads) + len(stores)])
+        made.start()
+        stores.append(made)
+        pair_stores.append(links.start(src, dst, sib))
+
+    def store_unit(n):
+        if n < 4:
+            store(outs[n], gup_out.at[c, n])
+        elif n < 8:
+            store(outs[n], gdown_out.at[c, n - 4])
+        elif n < 11:
+            store(outs[n], gqkv_out.at[c, n - 8])
+        else:
+            store(outs[n], gout_out.at[c])
+
+    units = [Unit(number) for number in range(12)]
+
+    steps, seen = [], [0] * len(units)
+    for group in EVENTS:
+        steps.append([])
+        for number in group:
+            steps[-1].append((number, seen[number]))
+            seen[number] += 1
+
+    def run(group):
+        for number, at in steps[group]:
+            units[number].advance(at)
+
+    beats = [0]
+
+    def beat():
+        run(beats[0])
+        beats[0] += 1
+
+    sem = backward_mlp(0, False)
+    for number in FIRST:
+        units[number].launch(0)
+    backward_norm(0, sem, beat)
+    first_group = beats[0]
+
+    def attention_round(i):
+        backward_heads(0, i)
+        for part in range(PARTS):
+            backward_part(0, i, part)
+            for turn in range(BLOCKS):
+                group = first_group + turn * PARTS + part
+                if steps[group]:
+                    pl.when(i == turn)(functools.partial(run, group))
+
+    each(0, BLOCKS, attention_round)
+    beats[0] += BLOCKS * PARTS
+    sem = backward_rest(0, False, beat)
+    for number in SECOND:
+        units[number].launch(0)
+    backward_end(sem)
+
+    def add_halt(i):
+        g[base + i] = g[base + i] + glog[i] * w_halt
+
+    each(0, PAIR, add_halt)
+    ig_s[...] = g[flip(z, 2), mine_rows, :].astype(BF)
+    ig_copy = links.start(ig_s, ig_r, to["2"])
+    for at in range(11):
+        small[at : at + 1, :] = colsum(acc[at * 8 : at * 8 + 8, :])
+    small_now = small
+    last = list(steps[beats[0]])
+    for number, d in enumerate("xy2"):
+        made = links.start(small_now, smallx.at[2 * number], to[d])
+        for _ in range(6):
+            unit, at = last.pop(0)
+            units[unit].advance(at)
+        made.wait_recv()
+        smallx[2 * number + 1] = small_now[...] + smallx[2 * number]
+        small_now = smallx.at[2 * number + 1]
+    small_out[c] = small_now[...]
+    small_pair = links.start(small_now, small_out.at[c], sib)
+    ig_copy.wait_recv()
+    igrad_out[...] = g[z, mine_rows, :] + ig_r[...].astype(F32)
+    for unit, at in last:
+        units[unit].advance(at)
+    small_pair.wait_recv()
+    for made in stores:
+        made.wait()
+    for made in pair_stores:
+        made.wait_recv()
+    for unit in units:
+        unit.drain()
+    links.drain()
+
+
+def fused_scratch():
+    v = pltpu.VMEM
+    dma = pltpu.SemaphoreType.DMA
+    f = lambda *shape: v(shape, F32)
+    h = lambda *shape: v(shape, BF)
+    grads = [f(2, 2, 2, r, k) for r, k in UNITS]
+
+    def parts():
+        made = []
+        for (r, k), (reduce, _) in zip(UNITS, PLAN):
+            left, stages = [2, 2, 2], []
+            for dims in map(axes_of, reduce):
+                left = left[len(dims) :]
+                stages.append([h(*left, r, k) for _ in range(2 ** len(dims) - 1)])
+            made.append(stages)
+        return made
+
+    return [
+        dma((N_LINKS,)), dma((N_LINKS,)), dma((32,)),
+        h(WIDE, 3 * FEAT), h(FEAT, WIDE), h(WIDE, HALF), h(HALF, WIDE),
+        h(BLOCKS, 2, TOK, WIDE), h(PAIR, 2, TOK, WIDE), f(PAIR, 2, TOK, 128), f(SEQ, 256),
+        h(BLOCKS, ROWS, WIDE), f(BLOCKS, ROWS, WIDE),
+        h(2, BLOCKS, ROWS, FEAT), h(2, BLOCKS, ROWS, FEAT), h(FEAT, SEQ), h(FEAT, SEQ),
+        h(SAVED, ROWS, FEAT), h(QROWS, FEAT), h(QROWS, FEAT),
+        f(SEQ, WIDE), h(SEQ, WIDE), f(SAVED, 1, QROWS), f(SAVED, FEAT, ROWS), h(FEAT, SAVED * ROWS),
+        f(SAVED, ROWS, WIDE), f(SAVED, ROWS, WIDE), f(SAVED, ROWS, 1), f(SAVED, ROWS, 1),
+        h(SAVED, ROWS, WIDE), h(SAVED, ROWS, HALF), h(SAVED, ROWS, HALF),
+        h(2 * BLOCKS, ROWS, WIDE), h(2 * BLOCKS, ROWS, WIDE),
+        f(BLOCKS, ROWS, WIDE), h(BLOCKS, ROWS, WIDE), h(BLOCKS, ROWS, HALF),
+        f(SEQ, FEAT), f(SEQ, FEAT), f(FEAT, ROWS), f(1, QROWS), h(BLOCKS, ROWS, 3 * FEAT),
+        f(2, PAIR, ROWS, 1), f(PAIR, ROWS, 1), f(88, WIDE), f(16, WIDE), f(6, 16, WIDE), h(TOK, WIDE), h(TOK, WIDE),
+        grads, parts(), parts(),
+        [h(2, 2, 2, 2, r, k) for r, k in UNITS],
+    ]
+
+
+BIG = ((WIDE, 3 * WIDE), (WIDE, WIDE), (WIDE, 2 * HALF), (2 * HALF, WIDE))
+
+
+def widen_kernel(gqkv, gout, gup, gdown, small, final, igrad,
+                 o_final, o_igrad, o_qkv, o_qv, o_out, o_ob, o_up, o_ub, o_down, o_db, o_gain, o_shift, o_hw, o_hb,
+                 narrow, wide, read_sem, write_sem):
+    half = lambda at: BIG[at][0] // 2
+    groups = []
+    for core in range(2):
+        rows = pl.ds(core * HALF, HALF)
+        groups.append(([(gdown.at[core, k], narrow[3].at[rows, pl.ds(k * 128, 128)]) for k in range(4)],
+                       [(3, rows)]))
+    both = lambda at: [(at, pl.ds(0, half(at))), (at, pl.ds(half(at), half(at)))]
+    groups.append(([(gup.at[core, k, b], narrow[2].at[:, pl.ds(core * HALF + b * WIDE + k * 128, 128)])
+                    for core in range(2) for k in range(4) for b in range(2)], both(2)))
+    groups.append(([(gqkv.at[core, k], narrow[0].at[:, pl.ds(k * WIDE + core * FEAT, FEAT)])
+                    for core in range(2) for k in range(3)], both(0)))
+    groups.append(([(gout, narrow[1])], [(1, pl.ds(0, WIDE))]))
+    results = (o_qkv, o_out, o_up, o_down)
+    reads, writes = [], []
+    count = 0
+    for sources, _ in groups:
+        some = []
+        for src, dst in sources:
+            made = pltpu.make_async_copy(src, dst, read_sem.at[count])
+            count += 1
+            made.start()
+            some.append(made)
+        reads.append(some)
+    for some, (_, pieces) in zip(reads, groups):
+        for made in some:
+            made.wait()
+        for at, rows in pieces:
+            wide[at][rows, :] = narrow[at][rows, :].astype(F32)
+            made = pltpu.make_async_copy(wide[at].at[rows, :], results[at].at[rows, :], write_sem.at[len(writes)])
+            made.start()
+            writes.append(made)
+    o_final[...] = final[...]
+    o_igrad[...] = igrad[...]
+    a, b = small[0], small[1]
+    row = lambda v, i: v[i : i + 1, :]
+    o_qv[0:1, :FEAT] = a[0:1, :FEAT]
+    o_qv[0:1, FEAT:] = b[0:1, :FEAT]
+    o_qv[1:2, :FEAT] = a[0:1, FEAT:]
+    o_qv[1:2, FEAT:] = b[0:1, FEAT:]
+    o_ob[...] = row(a, 1).reshape(WIDE)
+    for k, v in enumerate((a, b)):
+        for j in range(2):
+            o_ub[pl.ds((2 * k + j) * WIDE, WIDE)] = row(v, 2 + j).reshape(WIDE)
+    o_db[...] = row(a, 4).reshape(WIDE)
+    o_gain[...] = a[5:7, :]
+    o_shift[...] = a[7:9, :]
+    o_hw[...] = row(a, 9).reshape(WIDE)
+    o_hb[...] = row(a, 10)[:, :128].reshape(128)
+    for made in writes:
+        made.wait()
+
+
+def widen(final, igrad, small, gqkv, gout, gup, gdown):
+    shapes = [
+        (TOK, WIDE), (TOK, WIDE), BIG[0], (2, WIDE), BIG[1], (WIDE,), BIG[2], (2 * HALF,), BIG[3], (WIDE,),
+        (2, WIDE), (2, WIDE), (WIDE,), (128,),
+    ]
+    vm = pl.BlockSpec(memory_space=pltpu.VMEM)
+    hbm = pl.BlockSpec(memory_space=pl.ANY)
+    return pl.pallas_call(
+        widen_kernel,
+        out_shape=tuple(jax.ShapeDtypeStruct(a, F32) for a in shapes),
+        in_specs=[hbm] * 4 + [vm] * 3,
+        out_specs=tuple(hbm if a in BIG else vm for a in shapes),
+        scratch_shapes=[
+            [pltpu.VMEM(a, BF) for a in BIG],
+            [pltpu.VMEM(a, F32) for a in BIG],
+            pltpu.SemaphoreType.DMA((32,)),
+            pltpu.SemaphoreType.DMA((8,)),
+        ],
+        compiler_params=pltpu.CompilerParams(vmem_limit_bytes=62 * 2**20),
+        name="widen",
+    )(gqkv.reshape(2, 3, WIDE, FEAT), gout.reshape(BIG[1]), gup.reshape(2, 4, 2, WIDE, 128),
+      gdown.reshape(2, 4, HALF, 128), small, final, igrad)
+
+
+def fused_local(
+    states, w_qkv, qv_bias, output_weight, out_bias, w_up, up_bias, w_down, down_bias,
+    norm_gain, norm_shift, halt_weight, halt_bias, cotangent, lengths, caps,
+):
+    vm = pl.BlockSpec(memory_space=pltpu.VMEM)
+    sm = pl.BlockSpec(memory_space=pltpu.SMEM)
+    hbm = pl.BlockSpec(memory_space=pl.ANY)
+    out = lambda *shape: jax.ShapeDtypeStruct(shape, BF)
+    made = pl.pallas_call(
+        fused_kernel,
+        out_shape=(
+            jax.ShapeDtypeStruct((TOK, WIDE), F32),
+            jax.ShapeDtypeStruct((TOK, WIDE), F32),
+            jax.ShapeDtypeStruct((2, 16, WIDE), F32),
+            out(2, 3, 2, 2, 2, 2, *UNITS[8]),
+            out(2, 2, 2, 2, 2, *UNITS[11]),
+            out(2, 4, 2, 2, 2, 2, *UNITS[0]),
+            out(2, 4, 2, 2, 2, 2, *UNITS[4]),
+        ),
+        in_specs=[vm] * 3 + [sm] + [vm] * 7 + [sm] + [hbm] * 4,
+        out_specs=[vm] * 3 + [hbm] * 4,
+        scratch_shapes=fused_scratch(),
+        compiler_params=pltpu.CompilerParams(
+            collective_id=0, has_side_effects=True, vmem_limit_bytes=64 * 2**20 - 2**18
+        ),
+        name="ponder",
+    )(states[0], cotangent[0], caps, lengths, qv_bias, out_bias, up_bias, down_bias, norm_gain, norm_shift,
+      halt_weight, halt_bias, w_qkv, output_weight, w_up, w_down)
+    final, igrad, gqkv, grad_qv, gout, g_ob, gup, g_ub, gdown, g_db, gain, shift, g_hw, g_hb = widen(*made)
+    return (
+        final[None], igrad[None], gqkv, grad_qv, gout, g_ob, gup, g_ub, gdown, g_db, gain, shift, g_hw, g_hb[:1]
+    )
+
+
+SPECS_IN = (P("dp", "seq", None),) + (P(),) * 12 + (P("dp", "seq", None), P("dp"), P("dp", "seq"))
+SPECS_OUT = (P("dp", "seq", None),) * 2 + (P(),) * 12
+
+
 def solution(mesh):
-    return jax.shard_map(
-        local,
-        mesh=mesh,
-        in_specs=(
-            P("dp", "seq", None),
-            P(),
-            P(),
-            P(),
-            P(),
-            P(),
-            P(),
-            P(),
-            P(),
-            P(),
-            P(),
-            P(),
-            P(),
-            P("dp", "seq", None),
-            P("dp"),
-            P("dp", "seq"),
-        ),
-        out_specs=(
-            P("dp", "seq", None),
-            P("dp", "seq", None),
-            P(),
-            P(),
-            P(),
-            P(),
-            P(),
-            P(),
-            P(),
-            P(),
-            P(),
-            P(),
-            P(),
-            P(),
-        ),
-        check_vma=False,
-    )
+    square = mesh.shape["dp"] == 4 and mesh.shape["seq"] == 2 * BLOCKS
+
+    def whole(*arrays):
+        states, w_up = arrays[0], arrays[5]
+        fits = square and states.shape == (4, SEQ, WIDE) and w_up.shape == (WIDE, 2 * HALF)
+        return jax.shard_map(
+            fused_local if fits else local,
+            mesh=mesh,
+            in_specs=SPECS_IN,
+            out_specs=SPECS_OUT,
+            check_vma=False,
+        )(*arrays)
+
+    return whole

time: 609 us -> 137 us (0.22)
  waiting for transfers between devices: 400 us -> 0 us
  Pallas kernels: 0 us -> 135 us
  local copies, waits for them, and re-layouts: 63.5 us -> 0 us
  matrix products: 51.9 us -> 0 us
  blocking collectives: 43.6 us -> 0 us
  other arithmetic: 29.8 us -> 0 us
  between operations: 16.1 us -> 2.13 us
    psum x1 -> x0, waiting for transfers between devices: 190 us -> none  [local(): lax.psum((totals[0], totals[1], totals[2], totals[3], totals[4], totals[5...]
    pallas_call x0 -> x2, Pallas kernels: none -> 135 us  [the longest x1 127 us: fused_local(): pl.pallas_call(fused_kernel, out_shape=(jax.ShapeDtypeStruct((TOK, WIDE),...]
    reduce_scatter x4 -> x0, waiting for transfers between devices: 124 us -> none  [the longest x2 70.8 us: attend_back(): lax.psum_scatter(grad_key_all, 'seq', scatter_dimension=1, tiled=True)]
    all_gather x4 -> x0, waiting for transfers between devices: 84.9 us -> none  [the longest x2 44 us: attend(): key_piece = lax.all_gather(key_rows, 'seq', axis=1, tiled=True)]
    dot_general x52 -> x0, matrix products: 51.9 us -> none  [the longest x8 5.57 us: one_block(): jnp.einsum('sqhe,skhe->shqk', query_heads, key_block, preferred_element_t...]
    psum x1 -> x0, blocking collectives: 43.6 us -> none  [local(): lax.psum((totals[0], totals[1], totals[2], totals[3], totals[4], totals[5...]
    unnamed x274 -> x0, local copies, waits for them, and re-layouts: 25 us -> none
    reduce_sum x26 -> x0, other arithmetic: 15.9 us -> none  [the longest x2 3.82 us: backward_block(): jnp.sum(grad_mixed[..., 2 * model_width:].astype(jnp.float32), axis=(0, 1))]
  transfers between devices with their start and end apart: 9 -> 0, of which waited for: 9 -> 0; matrix products, arithmetic and copies ran while one was open for 4% -> 0% of each run, Pallas kernels for 0% -> 0%
where the time goes in v2:
time: 137 us
  Pallas kernels  135 us (99%)
  between operations  2.13 us (2%)
    pallas_call x1, Pallas kernels, fused_local(): pl.pallas_call(fused_kernel, out_shape=(jax.ShapeDtypeStruct((TOK, WIDE),...  127 us
    pallas_call x1, Pallas kernels, widen(): pl.pallas_call(widen_kernel, out_shape=tuple((jax.ShapeDtypeStruct(a, F32...  8.1 us

profile of v2, /device:TPU:1, one launch (start us, length us, event | category | flops | bytes accessed | tf_op | source)
XLA Modules:
  0.0 137.1 jit_solution(16396656280901431423)
XLA Ops:
  1.9 126.9 %ponder.1 = (f32[128,512]{1,0:T(8,128)}, f32[128,512]{1,0:T(8,128)}, f32[2,16,512]{2,1,0:T(8,128)}, bf16[2,3,2,2,2,2,32,256]{7,6,5,4,3,2,1,0:T(8,128)(2,1)}, bf1...) custom-call(bf16[128,512]{1,0:T(8,128)(2,1)} %bitcast.13, ...), custom_call_target="tpu_custom_call" | custom-call | tf_op jit(solution)/shard_map/ponder/pallas_call | solution.py:1293
  128.8 8.1 %widen.1 = (f32[128,512]{1,0:T(8,128)}, f32[128,512]{1,0:T(8,128)}, f32[512,1536]{1,0:T(8,128)}, f32[2,512]{1,0:T(2,128)}, f32[512,512]{1,0:T(8,128)}, /*index=5...) custom-call(bf16[2,3,512,256]{3,2,1,0:T(8,128)(2,1)} %bitcast.11, ...), custom_call_target="tpu_custom_call" | custom-call | tf_op jit(solution)/shard_map/widen/pallas_call | solution.py:1268
